TPU v7x, 128 devices: a whole 4x4x4 slice. The times are simulated.
128 devices in a mesh: gx: 8 (over y, core), gy: 16 (over x, z).
Axes of the slice: x: 4, y: 4, z: 4, core: 2. Of those that a mesh axis runs over, the one named last changes fastest.
Arguments:
- a_blocks: bfloat16 [3072, 7, 256, 256], P(('gx', 'gy'))
- prolong: bfloat16 [3072, 256, 128], P(('gx', 'gy'))
- neighbour: int32 [3072, 6], P(('gx', 'gy')), may hold values from 0 to 71, as said below
- ghost_send: int32 [8, 16, 16, 3], P('gx', 'gy'), may hold values from 0 to 23
- fine_agg: int32 [3072], P(('gx', 'gy')), may hold values from 0 to 255, as said below
- balance: int32 [8, 16, 16], P('gx', 'gy'), may hold values from 0 to 128, as said below
- coarse_cols: int32 [1024, 7], P(('gx', 'gy')), may hold values from 0 to 1023, as said below
- loads: bfloat16 [1024, 128, 256], P(('gx', 'gy')), may hold values from -48 to 48
Outputs:
- coarse: bfloat16 [1024, 7, 128, 128], P(('gx', 'gy'))
- smoothed: bfloat16 [1024, 128, 256], P(('gx', 'gy'))
Inputs may be any that keep to these rules, and one draw needn't show every extreme that they name: `neighbour`: an entry below 24 names a block row of the same device. An entry v >= 24 names slot (v - 24) % 3 of the blocks sent by the device of the same gx row at gy index (v - 24) // 3, never the device itself; every slot so named is named at least once, and the slots named from one peer are the first few of its 3; some device names all 3 slots of some peer. `fine_agg`: the owner is a device of the same gx row. Each aggregate is named by exactly three fine block rows, on three different devices. At most 3 block rows of one device name aggregates of one owner, and this is reached in every draw. Every named slot has a balance entry below 128, and some owner holds 16 aggregates. `balance`: entry 128 marks a slot that no block row names. Every coarse row of a gx row receives exactly one slot, and one owner sends at most one aggregate to each device. At most 3 block rows of one device have their target coarse row on one device, and this is reached in every draw. coarse_cols[g, 0] = g; the other entries name coarse rows of the same device or of a device whose gy index differs by one, in the same gx row.
All inputs are finite; a program needn't handle non-finite values.
Results may differ from a plain program's by a relative error of at most 0.0051.
Values may be sent and summed in bfloat16 or wider, within the bound.
A program may use at most 128 MiB of HBM per device.

v0:
```python
import jax
import jax.numpy as jnp
from jax import lax
from jax.sharding import PartitionSpec as P

OCAP = 3
SWEEPS = 2


def padded_2(block, sides, width):
    for axis, dim in sides:
        count = lax.axis_size(axis)
        forward = [(i, i + 1) for i in range(count - 1)]
        backward = [(target, source) for source, target in forward]
        low = lax.ppermute(
            lax.slice_in_dim(block, block.shape[dim] - width, None, axis=dim), axis, forward
        )
        high = lax.ppermute(lax.slice_in_dim(block, 0, width, axis=dim), axis, backward)
        block = jnp.concatenate([low, block, high], axis=dim)
    return block


def rank_within(labels, label_count):
    one_hot = (labels[:, None] == jnp.arange(label_count, dtype=jnp.int32)[None, :]).astype(
        jnp.int32
    )
    running = jnp.cumsum(one_hot, axis=0) - one_hot
    return jnp.sum(running * one_hot, axis=1)


def place_rows(values, tag_values, positions, capacity, empty_tag):
    buffer = (
        jnp.zeros((capacity,) + values.shape[1:], values.dtype)
        .at[positions]
        .set(values, mode="drop")
    )
    labels = jnp.full((capacity,), empty_tag, jnp.int32).at[positions].set(tag_values, mode="drop")
    return (buffer, labels)


def sum_tagged(values, labels, label_count):
    selector = (jnp.arange(label_count, dtype=jnp.int32)[:, None] == labels[None, :]).astype(
        values.dtype
    )
    return jnp.einsum("ts,skab->tkab", selector, values, preferred_element_type=jnp.float32)


def per_device(a_blocks, prolong, neighbour, ghost_send, fine_agg, balance, coarse_cols, loads):
    block_rows = a_blocks.shape[0]
    group_size = lax.axis_size("gy")
    row_gy = lax.axis_index("gy")
    row_gx = lax.axis_index("gx")
    everyone, send_lists = (
        lax.all_gather(prolong, "gy", axis=0, tiled=True),
        lax.all_gather(ghost_send, "gy", axis=1, tiled=True),
    )
    wanted = send_lists[0, :, row_gy, :]
    pool_index = jnp.arange(group_size, dtype=jnp.int32)[:, None] * block_rows + wanted
    block_pool = jnp.concatenate([prolong, everyone[pool_index.reshape(-1)]], axis=0)
    self_index = jnp.arange(block_rows, dtype=jnp.int32)[:, None]
    columns = jnp.concatenate([self_index, neighbour], axis=1)
    right_blocks = block_pool[columns]
    applied = jnp.einsum(
        "ikab,ikbc->ikac", a_blocks, right_blocks, preferred_element_type=jnp.float32
    ).astype(jnp.bfloat16)
    partial_value = jnp.einsum(
        "iac,ikad->ikcd", prolong, applied, preferred_element_type=jnp.float32
    ).astype(jnp.bfloat16)
    slot_count = balance.shape[2]
    coarse_rows = loads.shape[0]
    owner_dev = fine_agg // slot_count
    slot_index = fine_agg % slot_count
    placing = owner_dev * OCAP + rank_within(owner_dev, group_size)
    buffer, labels = place_rows(partial_value, slot_index, placing, group_size * OCAP, slot_count)
    received, received_labels = (
        lax.all_to_all(buffer, "gy", split_axis=0, concat_axis=0, tiled=True),
        lax.all_to_all(labels, "gy", split_axis=0, concat_axis=0, tiled=True),
    )
    held_rows = sum_tagged(received, received_labels, slot_count).astype(jnp.bfloat16)
    destination = balance[0, 0]
    peer_index = destination // coarse_rows
    within = destination % coarse_rows
    moving, moving_labels = place_rows(held_rows, within, peer_index, group_size, coarse_rows)
    arrived_rows, arrived_labels = (
        lax.all_to_all(moving, "gy", split_axis=0, concat_axis=0, tiled=True),
        lax.all_to_all(moving_labels, "gy", split_axis=0, concat_axis=0, tiled=True),
    )
    coarse = sum_tagged(arrived_rows, arrived_labels, coarse_rows).astype(jnp.bfloat16)
    magnitude = jnp.sum(jnp.abs(coarse.astype(jnp.float32)), axis=(1, 3))
    largest = lax.pmax(jnp.max(magnitude), ("gx", "gy"))
    lower_end = largest / 30.0
    centre = (largest + lower_end) / 2.0
    half_width = (largest - lower_end) / 2.0
    sigma_ratio = centre / half_width
    right_side = loads.astype(jnp.float32)
    solution = right_side / centre
    update = solution
    weight_now = 1.0 / sigma_ratio
    first_col = (row_gx * group_size + row_gy - 1) * coarse_rows
    local_cols = coarse_cols - first_col
    for sweep_index in range(SWEEPS):
        rounded = solution.astype(jnp.bfloat16)
        padded = padded_2(rounded, (("gy", 0),), coarse_rows)
        picked = padded[local_cols]
        product = jnp.einsum("rkab,rkbl->ral", coarse, picked, preferred_element_type=jnp.float32)
        residual = right_side - product
        weight_next = 1.0 / (2.0 * sigma_ratio - weight_now)
        update = weight_next * weight_now * update + 2.0 * weight_next / half_width * residual
        solution = solution + update
        weight_now = weight_next
    return (coarse, solution.astype(jnp.bfloat16))


def solution(mesh):
    return jax.shard_map(
        per_device,
        mesh=mesh,
        in_specs=(
            P(("gx", "gy"), None, None, None),
            P(("gx", "gy"), None, None),
            P(("gx", "gy"), None),
            P("gx", "gy", None, None),
            P(("gx", "gy")),
            P("gx", "gy", None),
            P(("gx", "gy"), None),
            P(("gx", "gy"), None, None),
        ),
        out_specs=(P(("gx", "gy"), None, None, None), P(("gx", "gy"), None, None)),
        check_vma=False,
    )
```

profile of v0, /device:TPU:1, one launch (start us, length us, event | category | flops | bytes accessed | tf_op | source)
XLA Modules:
  0.0 659.4 jit_solution(9548056900163910471)
XLA Ops:
  10.2 8.4 %all-to-all-start.1 = ((s32[16,3,1]{1,2,0:T(1,128)}), s32[16,3,1]{1,2,0:T(1,128)S(1)}, u32[]{:S(2)}, u32[]{:S(2)}) async-start(s32[16,3,1]{1,2,0:T(1,128)} %bitcast.6), calls=%async_computation.1 | async-start | bytes 16384 | tf_op jit(solution)/shard_map/all_to_all | solution.py:77
  18.7 19.6 %all_gather.7 = s32[1,16,16,3]{2,0,3,1:T(1,128)S(1)} all-gather(s32[1,1,16,3]{2,0,3,1:T(1,128)} %bitcast.78), channel_id=1, replica_groups=mesh['gx'=8,'gy'=16] {'gy'}, dimensions={1}, use_global_device_ids=true | all-gather | bytes 3264 | tf_op jit(solution)/shard_map/all_gather | solution.py:55
  40.5 127.4 %all-gather.2.cloned.1.call-done = bf16[384,256,128]{2,1,0:T(8,128)(2,1)} async-done(((bf16[24,256,128]{2,1,0:T(8,128)(2,1)}), bf16[384,256,128]{2,1,0:T(8,128)(2,1)}) %all-gather.2.cloned.1.call-update) | async-done | bytes 25165840 | tf_op jit(solution)/shard_map/all_gather | solution.py:54
  167.9 11.0 %gather_fusion = bf16[48,256,128]{2,1,0:T(8,128)(2,1)} fusion(bf16[384,256,128]{2,1,0:T(8,128)(2,1)} %all-gather.2.cloned.1.call-done, s32[1024]{0:T(1024)S(1)} %pad_clamp_fusion.2), kind=kCustom, calls=%fused_computation | custom fusion | bytes 6291648 | tf_op jit(solution)/shard_map/gather | solution.py:59
  178.9 4.5 pad_maximum_fusion
  183.4 10.1 %gather_fusion.1 = bf16[168,256,128]{2,1,0:T(8,128)(2,1)} fusion(bf16[72,256,128]{2,1,0:T(8,128)(2,1)} %pad_maximum_fusion, s32[1024]{0:T(1024)S(1)} %pad_clamp_fusion.1), kind=kCustom, calls=%fused_computation.1 | custom fusion | bytes 22020768 | tf_op jit(solution)/shard_map/gather | solution.py:62
  193.5 18.1 %convert_bitcast_fusion = bf16[24,7,128,128]{2,3,1,0:T(8,128)(2,1)} fusion(bf16[24,7,256,128]{3,2,1,0:T(8,128)(2,1)} %bitcast.74, bf16[24,7,256,256]{3,2,1,0:T(8,128)(2,1)} %param.8, bf16[24,256,128]{2,1,0:T(8,128)(2,1)S(1)} %copy-done), kind=kOutput, calls=%fused_computation.14 | convolution fusion | flops 4236115968 | bytes 40108032 | tf_op jit(solution)/shard_map/iac,ikad->ikcd/dot_general | solution.py:66
  211.6 8.3 %copy.49 = bf16[24,7,128,128]{3,2,1,0:T(8,128)(2,1)} copy(bf16[24,7,128,128]{2,3,1,0:T(8,128)(2,1)} %convert_bitcast_fusion) | data formatting | bytes 11010048 | tf_op jit(solution)/shard_map/convert_element_type | solution.py:68
  219.9 7.0 %broadcast_in_dim.13 = bf16[48,7,128,128]{3,2,1,0:T(8,128)(2,1)} broadcast(bf16[]{:T(256)} %constant.88.clone.1), dimensions={} | broadcast | bytes 11010050 | tf_op jit(solution)/shard_map/broadcast_in_dim | solution.py:33
  226.9 16.1 %scatter_fusion = bf16[48,7,128,128]{3,2,1,0:T(8,128)(2,1)} fusion(bf16[48,7,128,128]{3,2,1,0:T(8,128)(2,1)} %broadcast_in_dim.13, s32[24]{0:T(128)S(1)} %compare_select_fusion.3, bf16[24,7,128,128]{3,2,1,0:T(8,128)(2,1)} %copy.49), kind=kCustom, calls=%fused_computation.6 | custom fusion | bytes 16515168 | tf_op jit(solution)/shard_map/scatter | solution.py:35
  243.0 5.1 all-to-all-start.2
  250.8 188.1 %all-to-all-done.2 = bf16[48,7,128,128]{3,2,1,0:T(8,128)(2,1)} async-done(((bf16[48,7,128,128]{3,2,1,0:T(8,128)(2,1)}), bf16[48,7,128,128]{3,2,1,0:T(8,128)(2,1)}, u32[]{:S(2)}, u32[]{:S(2)}) %all-to-all-start.2) | async-done | bytes 11010080 | tf_op jit(solution)/shard_map/all_to_all | solution.py:76
  438.9 12.6 %all-to-all-start = ((s32[16,1,1]{2,1,0:T(1,128)}), s32[16,1,1]{2,1,0:T(1,128)S(1)}, u32[]{:S(2)}, u32[]{:S(2)}) async-start(s32[16,1,1]{2,1,0:T(1,128)} %copy.44), calls=%async_computation | async-start | bytes 16384 | tf_op jit(solution)/shard_map/all_to_all | solution.py:86
  451.4 10.5 %fusion.11 = bf16[16,7,128,128]{3,0,2,1:T(8,128)(2,1)S(1)} fusion(bf16[48,7,128,128]{3,2,1,0:T(8,128)(2,1)} %all-to-all-done.2, s32[48]{0:T(128)S(1)} %eq.55), kind=kOutput, calls=%fused_computation.19 | convolution fusion | flops 177996544 | bytes 14680256 | tf_op jit(solution)/shard_map/ts,skab->tkab/dot_general | solution.py:45
  467.4 8.2 %scatter_fusion.1 = bf16[16,7,128,128]{3,2,1,0:T(8,128)(2,1)} fusion(bf16[16,7,128,128]{3,2,1,0:T(8,128)(2,1)} %broadcast_in_dim.10, s32[16]{0:T(128)S(1)} %fusion.32, bf16[16,7,128,128]{3,2,1,0:T(8,128)(2,1)} %copy.51), kind=kCustom, calls=%fused_computation.7 | custom fusion | bytes 11010112 | tf_op jit(solution)/shard_map/scatter | solution.py:35
  475.7 8.4 %all-to-all-start.3 = ((bf16[16,7,128,128]{3,2,1,0:T(8,128)(2,1)}), bf16[16,7,128,128]{3,2,1,0:T(8,128)(2,1)}, u32[]{:S(2)}, u32[]{:S(2)}) async-start(bf16[16,7,128,128]{3,2,1,0:T(8,128)(2,1)} %scatter_fusion.1), calls=%async_computation.3 | async-start | bytes 7340032 | tf_op jit(solution)/shard_map/all_to_all | solution.py:85
  484.5 40.5 %all-to-all-done.3 = bf16[16,7,128,128]{3,2,1,0:T(8,128)(2,1)} async-done(((bf16[16,7,128,128]{3,2,1,0:T(8,128)(2,1)}), bf16[16,7,128,128]{3,2,1,0:T(8,128)(2,1)}, u32[]{:S(2)}, u32[]{:S(2)}) %all-to-all-start.3) | async-done | bytes 3670048 | tf_op jit(solution)/shard_map/all_to_all | solution.py:85
  525.0 5.8 abs_reduce_fusion
  531.4 71.5 %pmax.7 = f32[]{:T(128)} all-reduce(f32[]{:T(128)} %reduce_max.9), channel_id=1, replica_groups=mesh['gx'=8,'gy'=16] {'gx','gy'}, use_global_device_ids=true, to_apply=%region_8.9 | all-reduce | flops 1 | bytes 8 | tf_op jit(solution)/shard_map/pmax | solution.py:90
  612.5 4.9 collective-permute-done
  617.4 3.8 collective-permute-done.1
  624.0 4.0 fusion.23
  632.2 8.0 %collective-permute-done.2 = bf16[8,128,256]{2,1,0:T(8,128)(2,1)S(1)} collective-permute-done((bf16[8,128,256]{2,1,0:T(8,128)(2,1)S(1)}, bf16[8,128,256]{2,1,0:T(8,128)(2,1)S(1)}, u32[]{:S(2)}, u32[]{:S(2)}) %collective-permute-start.2) | collective-permute-done | bytes 524320 | tf_op jit(solution)/shard_map/ppermute | solution.py:15
  648.4 4.2 add_convert_fusion
  (62 shorter events, 36.6 us)
Async XLA Ops:
  7.2 171.7 %copy-start = (bf16[24,256,128]{2,1,0:T(8,128)(2,1)S(1)}, bf16[24,256,128]{2,1,0:T(8,128)(2,1)}, u32[]{:S(2)}) copy-start(bf16[24,256,128]{2,1,0:T(8,128)(2,1)} %param.9) | copy-start | bytes 4718596
  7.2 160.7 %all-gather.2.cloned.1.call-start = ((), (), s32[]{:S(2)}) async-start(), calls=%async_computation.4 | async-start | bytes 26738688 | tf_op jit(solution)/shard_map/all_gather | solution.py:54
  10.2 232.8 %all-to-all-start.1 = ((s32[16,3,1]{1,2,0:T(1,128)}), s32[16,3,1]{1,2,0:T(1,128)S(1)}, u32[]{:S(2)}, u32[]{:S(2)}) async-start(s32[16,3,1]{1,2,0:T(1,128)} %bitcast.6), calls=%async_computation.1 | async-start | bytes 16384 | tf_op jit(solution)/shard_map/all_to_all | solution.py:77
  243.0 5.1 copy-start.6
  243.0 195.8 %all-to-all-start.2 = ((bf16[48,7,128,128]{3,2,1,0:T(8,128)(2,1)}), bf16[48,7,128,128]{3,2,1,0:T(8,128)(2,1)}, u32[]{:S(2)}, u32[]{:S(2)}) async-start(bf16[48,7,128,128]{3,2,1,0:T(8,128)(2,1)} %scatter_fusion), calls=%async_computation.2 | async-start | bytes 22020096 | tf_op jit(solution)/shard_map/all_to_all | solution.py:76
  438.9 36.8 %all-to-all-start = ((s32[16,1,1]{2,1,0:T(1,128)}), s32[16,1,1]{2,1,0:T(1,128)S(1)}, u32[]{:S(2)}, u32[]{:S(2)}) async-start(s32[16,1,1]{2,1,0:T(1,128)} %copy.44), calls=%async_computation | async-start | bytes 16384 | tf_op jit(solution)/shard_map/all_to_all | solution.py:86
  475.7 49.3 %all-to-all-start.3 = ((bf16[16,7,128,128]{3,2,1,0:T(8,128)(2,1)}), bf16[16,7,128,128]{3,2,1,0:T(8,128)(2,1)}, u32[]{:S(2)}, u32[]{:S(2)}) async-start(bf16[16,7,128,128]{3,2,1,0:T(8,128)(2,1)} %scatter_fusion.1), calls=%async_computation.3 | async-start | bytes 7340032 | tf_op jit(solution)/shard_map/all_to_all | solution.py:85
  484.1 120.1 %copy-start.2 = (bf16[8,128,256]{2,1,0:T(8,128)(2,1)S(1)}, bf16[8,128,256]{2,1,0:T(8,128)(2,1)}, u32[]{:S(2)}) copy-start(bf16[8,128,256]{2,1,0:T(8,128)(2,1)} %param.15) | copy-start | bytes 1572868
  484.1 124.3 %copy-start.5 = (s32[8,7]{1,0:T(8,128)S(1)}, s32[8,7]{1,0:T(8,128)}, u32[]{:S(2)}) copy-start(s32[8,7]{1,0:T(8,128)} %param.14) | copy-start | bytes 676
  604.4 13.0 %collective-permute-start = (bf16[8,128,256]{2,1,0:T(8,128)(2,1)S(1)}, bf16[8,128,256]{2,1,0:T(8,128)(2,1)S(1)}, u32[]{:S(2)}, u32[]{:S(2)}) collective-permute-start(bf16[8,128,256]{2,1,0:T(8,128)(2,1)S(1)} %fusion.22), channel_id=1, source_target_pairs={{0,1},{1,2},{2,3},{3,4},{4,5},{5,6},{6,7},{7,8},{8,9},{9,10},{10,1... | collective-permute-start | bytes 1572872 | tf_op jit(solution)/shard_map/ppermute | solution.py:15
  607.1 14.1 %collective-permute-start.1 = (bf16[8,128,256]{2,1,0:T(8,128)(2,1)S(1)}, bf16[8,128,256]{2,1,0:T(8,128)(2,1)S(1)}, u32[]{:S(2)}, u32[]{:S(2)}) collective-permute-start(bf16[8,128,256]{2,1,0:T(8,128)(2,1)S(1)} %fusion.22), channel_id=1, source_target_pairs={{1,0},{2,1},{3,2},{4,3},{5,4},{6,5},{7,6},{8,7},{9,8},{10,9},{11,1... | collective-permute-start | bytes 1572872 | tf_op jit(solution)/shard_map/ppermute | solution.py:18
  621.4 2.6 copy-start.1
  628.1 12.2 %copy-start.3 = (bf16[8,128,256]{2,1,0:T(8,128)(2,1)}, bf16[8,128,256]{2,1,0:T(8,128)(2,1)S(1)}, u32[]{:S(2)}) copy-start(bf16[8,128,256]{2,1,0:T(8,128)(2,1)S(1)} %get-tuple-element.16) | copy-start | bytes 1572868
  628.1 12.2 %collective-permute-start.2 = (bf16[8,128,256]{2,1,0:T(8,128)(2,1)S(1)}, bf16[8,128,256]{2,1,0:T(8,128)(2,1)S(1)}, u32[]{:S(2)}, u32[]{:S(2)}) collective-permute-start(bf16[8,128,256]{2,1,0:T(8,128)(2,1)S(1)} %get-tuple-element.16), channel_id=1, source_target_pairs={{0,1},{1,2},{2,3},{3,4},{4,5},{5,6},{6,7},{7,8},{8,9},{9,10},{10,1... | collective-permute-start | bytes 1572872 | tf_op jit(solution)/shard_map/ppermute | solution.py:15
  630.8 13.4 %collective-permute-start.3 = (bf16[8,128,256]{2,1,0:T(8,128)(2,1)S(1)}, bf16[8,128,256]{2,1,0:T(8,128)(2,1)}, u32[]{:S(2)}, u32[]{:S(2)}) collective-permute-start(bf16[8,128,256]{2,1,0:T(8,128)(2,1)S(1)} %get-tuple-element.16), channel_id=1, source_target_pairs={{1,0},{2,1},{3,2},{4,3},{5,4},{6,5},{7,6},{8,7},{9,8},{10,9},{11,1... | collective-permute-start | bytes 1572872 | tf_op jit(solution)/shard_map/ppermute | solution.py:18
  640.3 0.8 copy-start.4
Sparse Core Ops, SparseCore 0:
  10.2 157.6 all-gather.1
where the time goes:
time: 664 us; the launch traced here: 659 us
  waiting for transfers between devices  377 us (57%)
  blocking collectives  91.2 us (14%)
  local copies, waits for them, and re-layouts  80.3 us (12%)
  starting transfers between devices  42.6 us (6%)
  matrix products  42.6 us (6%)
  between operations  16.5 us (2%)
  other arithmetic  9.69 us (1%)
    all_to_all x1, waiting for transfers between devices, per_device(): lax.all_to_all(buffer, 'gy', split_axis=0, concat_axis=0, tiled=True)  188 us
    all_gather x1, waiting for transfers between devices, per_device(): lax.all_gather(prolong, 'gy', axis=0, tiled=True)  127 us
    pmax x1, blocking collectives, per_device(): largest = lax.pmax(jnp.max(magnitude), ('gx', 'gy'))  71.5 us
    all_to_all x1, waiting for transfers between devices, per_device(): lax.all_to_all(moving, 'gy', split_axis=0, concat_axis=0, tiled=True)  40.5 us
    scatter x2, local copies, waits for them, and re-layouts, place_rows(): buffer = jnp.zeros((capacity,) + values.shape[1:], values.dtype).at[posit...  24.4 us
    all_gather x1, blocking collectives, per_device(): lax.all_gather(ghost_send, 'gy', axis=1, tiled=True)  19.6 us
    dot_general x1, matrix products, per_device(): jnp.einsum('iac,ikad->ikcd', prolong, applied, preferred_element_type=jnp...  18.1 us
    dot_general x2, matrix products, sum_tagged(): jnp.einsum('ts,skab->tkab', selector, values, preferred_element_type=jnp....  16.3 us
  transfers between devices with their start and end apart: 9, of which 7 were waited for; matrix products, arithmetic and copies ran while one was open for 17% of the time, Pallas kernels for 0%

commit v1 on v0

v1 whole, which is shorter than its diff:
```python
import functools

import jax
import jax.numpy as jnp
from jax import lax
from jax.experimental import pallas as pl
from jax.experimental.pallas import tpu as pltpu
from jax.sharding import PartitionSpec as P

MESH = pl.DeviceIdType.MESH
NX = 4
NZ = 4
GCAP = 3
LINE = 12
SWEEPS = 2
CHUNKS = ((0, 3), (3, 6), (6, 7))
VMEM = pltpu.VMEM
SMEM = pltpu.SMEM
DMA = pltpu.SemaphoreType.DMA


def place():
    me = lax.axis_index("gy")
    return lax.axis_index("gx"), lax.div(me, NZ), lax.rem(me, NZ)


def line_peer(axis, step):
    gx, x, z = place()
    if axis == 0:
        return gx, lax.rem(x + step, NX) * NZ + z
    return gx, x * NZ + lax.rem(z + step, NZ)


def greet(peers):
    barrier = pltpu.get_barrier_semaphore()
    for peer in peers:
        pl.semaphore_signal(barrier, 1, device_id=peer, device_id_type=MESH)
    pl.semaphore_wait(barrier, len(peers))


def remote(src, dst, send, recv, peer):
    return pltpu.make_async_remote_copy(
        src_ref=src, dst_ref=dst, send_sem=send, recv_sem=recv, device_id=peer, device_id_type=MESH
    )


def ghost_kernel(
    prolong, sends, table, ghosts, tables, packed, held, own_sem,
    send1, recv1, send2, recv2, tsend1, trecv1, tsend2, trecv2, keep_sem, tkeep,
):
    gx, x, z = place()
    coords = (x, z)
    half = prolong.shape[1] // 2
    greet([line_peer(axis, step) for axis in (0, 1) for step in (1, 2, 3)])

    own_table = pltpu.make_async_copy(table, tables.at[x, z], tkeep.at[0])
    own_table.start()
    first = []
    for step in (1, 2, 3):
        copy = remote(table, tables.at[x, z], tsend1.at[step - 1], trecv1.at[step - 1], line_peer(0, step))
        copy.start()
        first.append(copy)

    started = []
    for step in (1, 2, 3, 0):
        for axis in (0, 1):
            near = lax.rem(coords[axis] + step, 4)

            def pack(n, carry, axis=axis, step=step, near=near):
                far, c = lax.div(n, GCAP), lax.rem(n, GCAP)
                peer = near * NZ + far if axis == 0 else far * NZ + near
                packed[axis, step, n] = prolong[sends[peer, c], axis * half : (axis + 1) * half, :]
                return carry

            lax.fori_loop(0, 4 * GCAP, pack, 0)
            if step:
                copy = remote(
                    packed.at[axis, step], held.at[axis, step - 1],
                    send1.at[axis, step - 1], recv1.at[axis, step - 1], line_peer(axis, step),
                )
                copy.start()
                started.append(copy)

    def rows(axis, px, pz):
        first_row = (px * NZ + pz) * GCAP
        return ghosts.at[pl.ds(first_row, GCAP), pl.ds(axis * half, half), :]

    def source_of(axis, back):
        near = lax.rem(coords[axis] + 4 - back, 4)
        return (near, z) if axis == 0 else (x, near)

    second = []
    kept = []
    for back in (0, 1, 2, 3):
        for axis in (0, 1):
            if back:
                remote(
                    packed.at[axis, back], held.at[axis, back - 1],
                    send1.at[axis, back - 1], recv1.at[axis, back - 1], line_peer(axis, back),
                ).wait_recv()
            at = packed.at[axis, 0] if back == 0 else held.at[axis, back - 1]
            px, pz = source_of(axis, back)
            for step in (1, 2, 3):
                far = lax.rem(coords[1 - axis] + step, 4)
                copy = remote(
                    at.at[pl.ds(far * GCAP, GCAP)], rows(axis, px, pz),
                    send2.at[axis, back, step - 1], recv2.at[axis, back, step - 1], line_peer(1 - axis, step),
                )
                copy.start()
                second.append(copy)
            copy = pltpu.make_async_copy(
                at.at[pl.ds(coords[1 - axis] * GCAP, GCAP)], rows(axis, px, pz), keep_sem.at[axis, back]
            )
            copy.start()
            kept.append(copy)
        if back == 0:
            own_table.wait()
        else:
            first[back - 1].wait_recv()
        px = lax.rem(x + 4 - back, 4)
        for step in (1, 2, 3):
            copy = remote(
                tables.at[px, z], tables.at[px, z],
                tsend2.at[back, step - 1], trecv2.at[back, step - 1], line_peer(1, step),
            )
            copy.start()
            second.append(copy)
    for copy in kept:
        copy.wait()
    for copy in started + first:
        copy.wait_send()
    for copy in second:
        copy.wait_send()
    for back in (0, 1, 2, 3):
        px = lax.rem(x + 4 - back, 4)
        for step in (1, 2, 3):
            pz = lax.rem(z + 4 - step, 4)
            remote(
                tables.at[px, pz], tables.at[px, pz],
                tsend2.at[back, step - 1], trecv2.at[back, step - 1], line_peer(1, step),
            ).wait_recv()
            for axis in (0, 1):
                near = lax.rem(coords[axis] + 4 - back, 4)
                far = lax.rem(coords[1 - axis] + 4 - step, 4)
                place_of = rows(axis, near, far) if axis == 0 else rows(axis, far, near)
                remote(
                    place_of, place_of,
                    send2.at[axis, back, step - 1], recv2.at[axis, back, step - 1], line_peer(1 - axis, step),
                ).wait_recv()


def exchange_ghosts(prolong, sends, table):
    rows, order, width = prolong.shape
    peers = NX * NZ
    return pl.pallas_call(
        ghost_kernel,
        out_shape=(
            jax.ShapeDtypeStruct((peers * GCAP, order, width), prolong.dtype),
            jax.ShapeDtypeStruct((NX, NZ, 8, 128), jnp.int32),
        ),
        in_specs=[
            pl.BlockSpec(memory_space=VMEM),
            pl.BlockSpec(memory_space=SMEM),
            pl.BlockSpec(memory_space=VMEM),
        ],
        out_specs=(pl.BlockSpec(memory_space=pl.ANY), pl.BlockSpec(memory_space=VMEM)),
        scratch_shapes=[
            VMEM((2, 4, 4 * GCAP, order // 2, width), prolong.dtype),
            VMEM((2, 3, 4 * GCAP, order // 2, width), prolong.dtype),
            DMA((1,)),
            DMA((2, 3)), DMA((2, 3)), DMA((2, 4, 3)), DMA((2, 4, 3)),
            DMA((3,)), DMA((3,)), DMA((4, 3)), DMA((4, 3)),
            DMA((2, 4)), DMA((1,)),
        ],
        compiler_params=pltpu.CompilerParams(
            collective_id=1, has_side_effects=True, vmem_limit_bytes=24 << 20
        ),
    )(prolong, sends, table)


def table_kernel(slots, coarse_rows, tables, packs, merges, count, number):
    gx, x, z = place()
    fine_rows = 24
    for half in (0, 1):
        def clear_merge(n, carry, half=half):
            merges[half, n] = 4 * LINE
            return carry

        def clear_pack(n, carry, half=half):
            packs[half, n] = 0
            return carry

        def clear_number(n, carry):
            number[n] = 0
            return carry

        lax.fori_loop(0, 4 * coarse_rows * 3, clear_merge, 0)
        lax.fori_loop(0, 4 * LINE, clear_pack, 0)
        lax.fori_loop(0, 4 * coarse_rows, clear_number, 0)
        mine = x if half == 0 else z

        def from_source(s, carry, half=half, mine=mine):
            dx, dz = (s, z) if half == 0 else (x, s)
            for n in range(4):
                count[n] = 0

            def one_row(i, inner):
                label = tables[dx, dz, 0, i]
                owner, slot = lax.div(label, slots), lax.rem(label, slots)
                target = tables[lax.div(owner, NZ), lax.rem(owner, NZ), 1, slot]
                device, row = lax.div(target, coarse_rows), lax.rem(target, coarse_rows)
                tx, tz = lax.div(device, NZ), lax.rem(device, NZ)
                near, far = (tx, tz) if half == 0 else (tz, tx)
                rank = count[near]
                count[near] = rank + 1

                @pl.when(near == mine)
                def _():
                    goal = far * coarse_rows + row
                    done = number[goal]
                    merges[half, goal * 3 + done] = s * LINE + rank
                    number[goal] = done + 1

                @pl.when(s == mine)
                def _():
                    packs[half, near * LINE + rank] = i

                return inner

            lax.fori_loop(0, fine_rows, one_row, 0)
            return carry

        lax.fori_loop(0, 4, from_source, 0)


def make_tables(tables, slots, coarse_rows):
    return pl.pallas_call(
        functools.partial(table_kernel, slots, coarse_rows),
        out_shape=(
            jax.ShapeDtypeStruct((2, 4 * LINE), jnp.int32),
            jax.ShapeDtypeStruct((2, 4 * coarse_rows * 3), jnp.int32),
        ),
        in_specs=[pl.BlockSpec(memory_space=SMEM)],
        out_specs=(pl.BlockSpec(memory_space=SMEM), pl.BlockSpec(memory_space=SMEM)),
        scratch_shapes=[SMEM((4,), jnp.int32), SMEM((4 * coarse_rows,), jnp.int32)],
    )(tables)


def product_kernel(neighbour, blocks, prolong, ghosts, partial, pool, applied, sems):
    i = pl.program_id(0)
    rows = prolong.shape[0]
    pieces, width = blocks.shape[1], prolong.shape[2]

    @pl.when(i == 0)
    def _():
        copies = [
            pltpu.make_async_copy(prolong, pool.at[pl.ds(0, rows)], sems.at[0]),
            pltpu.make_async_copy(ghosts, pool.at[pl.ds(rows, ghosts.shape[0])], sems.at[1]),
        ]
        for copy in copies:
            copy.start()
        for copy in copies:
            copy.wait()

    for k in range(pieces):
        column = i if k == 0 else neighbour[i, k - 1]
        applied[:, k * width : (k + 1) * width] = jnp.dot(
            blocks[0, k], pool[column], preferred_element_type=jnp.float32
        ).astype(applied.dtype)
    left = pool[i]
    result = lax.dot_general(
        left, applied[...], (((0,), (0,)), ((), ())), preferred_element_type=jnp.float32
    ).astype(partial.dtype)
    for k in range(pieces):
        partial[0, k] = result[:, k * width : (k + 1) * width]


def products(a_blocks, prolong, ghosts, neighbour):
    rows, pieces, order, _ = a_blocks.shape
    width = prolong.shape[2]
    pool = rows + ghosts.shape[0]
    return pl.pallas_call(
        product_kernel,
        grid_spec=pltpu.PrefetchScalarGridSpec(
            num_scalar_prefetch=1,
            grid=(rows,),
            in_specs=[
                pl.BlockSpec((1, pieces, order, order), lambda i, n: (i, 0, 0, 0)),
                pl.BlockSpec(memory_space=pl.ANY),
                pl.BlockSpec(memory_space=pl.ANY),
            ],
            out_specs=pl.BlockSpec((1, pieces, width, width), lambda i, n: (i, 0, 0, 0)),
            scratch_shapes=[
                VMEM((pool, order, width), prolong.dtype),
                VMEM((order, pieces * width), prolong.dtype),
                DMA((2,)),
            ],
        ),
        out_shape=jax.ShapeDtypeStruct((rows, pieces, width, width), prolong.dtype),
        compiler_params=pltpu.CompilerParams(
            dimension_semantics=("arbitrary",), vmem_limit_bytes=32 << 20
        ),
        cost_estimate=pl.CostEstimate(
            flops=2 * rows * pieces * order * width * (order + width),
            bytes_accessed=2 * rows * pieces * order * order,
            transcendentals=0,
        ),
    )(neighbour, a_blocks, prolong, ghosts)


def coarse_kernel(
    n_gx, partial, packs, merges, cols, loads, coarse, smoothed,
    low, high, pad0, pad1, state, change, peak, peaks,
    send1, recv1, send2, recv2, hsend, hrecv, psend, precv, *bufs,
):
    gx, x, z = place()
    gy = x * NZ + z
    coords = (x, z)
    count = NX * NZ
    width = partial.shape[2]
    half = width // 2
    rows = loads.shape[0]
    n_chunks = len(CHUNKS)
    out, pool, sums, back = (bufs[2 * n_chunks * n : 2 * n_chunks * (n + 1)] for n in range(4))
    up = (gx, lax.rem(gy + 1, count))
    down = (gx, lax.rem(gy + count - 1, count))
    across = [(lax.rem(gx + step, n_gx), gy) for step in range(1, n_gx)]
    lines = [line_peer(axis, step) for axis in (0, 1) for step in (1, 2, 3)]
    greet(lines + [up, down] + across)

    first = []
    for c, (k0, k1) in enumerate(CHUNKS):
        for step in (1, 2, 3, 0):
            for axis in (0, 1):
                b = 2 * c + axis
                near = lax.rem(coords[axis] + step, 4)

                def pack(n, carry, axis=axis, step=step, near=near, b=b, k0=k0, k1=k1):
                    value = partial[packs[axis, near * LINE + n], k0:k1, axis * half : (axis + 1) * half, :]
                    if step:
                        out[b][step - 1, n] = value
                    else:
                        pool[b][near * LINE + n] = value
                    return carry

                lax.fori_loop(0, LINE, pack, 0)
                if step:
                    copy = remote(
                        out[b].at[step - 1], pool[b].at[pl.ds(coords[axis] * LINE, LINE)],
                        send1.at[b, step - 1], recv1.at[b, step - 1], line_peer(axis, step),
                    )
                    copy.start()
                    first.append(copy)
                else:
                    pool[b][4 * LINE] = jnp.zeros(pool[b].shape[1:], pool[b].dtype)

    second = []
    for c, (k0, k1) in enumerate(CHUNKS):
        for axis in (0, 1):
            b = 2 * c + axis
            for step in (1, 2, 3):
                source = lax.rem(coords[axis] + 4 - step, 4)
                remote(
                    out[b].at[step - 1], pool[b].at[pl.ds(source * LINE, LINE)],
                    send1.at[b, step - 1], recv1.at[b, step - 1], line_peer(axis, step),
                ).wait_recv()
            for step in (1, 2, 3, 0):
                far = lax.rem(coords[1 - axis] + step, 4)

                def merge(r, carry, axis=axis, b=b, step=step, far=far, k0=k0, k1=k1):
                    at = (far * rows + r) * 3
                    terms = [merges[axis, at + n] for n in range(3)]
                    for k in range(k1 - k0):
                        total = pool[b][terms[0], k].astype(jnp.float32)
                        total += pool[b][terms[1], k].astype(jnp.float32)
                        total += pool[b][terms[2], k].astype(jnp.float32)
                        sums[b][step, r, k] = total.astype(jnp.bfloat16)
                    return carry

                lax.fori_loop(0, rows, merge, 0)
                if step:
                    copy = remote(
                        sums[b].at[step], back[b].at[step - 1],
                        send2.at[b, step - 1], recv2.at[b, step - 1], line_peer(1 - axis, step),
                    )
                    copy.start()
                    second.append(copy)

    halo = [
        remote(loads, low, hsend.at[0], hrecv.at[0], up),
        remote(loads, high, hsend.at[1], hrecv.at[1], down),
    ]
    for copy in halo:
        copy.start()

    for n, (c, (k0, k1)) in enumerate(list(enumerate(CHUNKS))):
        for axis in (0, 1):
            b = 2 * c + axis
            for step in (1, 2, 3):
                second[6 * c + 3 * axis + step - 1].wait_recv()

            def finish(r, carry, axis=axis, b=b, k0=k0, k1=k1):
                for k in range(k1 - k0):
                    total = sums[b][0, r, k].astype(jnp.float32)
                    for step in (1, 2, 3):
                        total += back[b][step - 1, r, k].astype(jnp.float32)
                    coarse[r, k0 + k, axis * half : (axis + 1) * half, :] = total.astype(jnp.bfloat16)
                return carry

            lax.fori_loop(0, rows, finish, 0)

    peak[...] = jnp.zeros(peak.shape, peak.dtype)

    def row_peak(r, carry):
        total = jnp.zeros((width, width), jnp.float32)
        for k in range(coarse.shape[1]):
            total += jnp.abs(coarse[r, k].astype(jnp.float32))
        top = jnp.max(jnp.sum(total, axis=1, keepdims=True), axis=0, keepdims=True)
        peak[0] = jnp.maximum(peak[0], jnp.broadcast_to(top, peak.shape[1:]))
        return carry

    lax.fori_loop(0, rows, row_peak, 0)

    base = 0
    for stage, peers in enumerate((lines[:3], lines[3:], across)):
        copies = []
        for n, peer in enumerate(peers):
            copy = remote(peak.at[stage], peaks.at[base + n], psend.at[base + n], precv.at[base + n], peer)
            copy.start()
            copies.append(copy)
        for copy in copies:
            copy.wait()
        top = peak[stage]
        for n in range(len(peers)):
            top = jnp.maximum(top, peaks[base + n])
        peak[stage + 1] = top
        base += len(peers)

    largest = peak[3, 0:1, 0:1]
    lower_end = largest / 30.0
    centre = (largest + lower_end) / 2.0
    half_width = (largest - lower_end) / 2.0
    sigma = centre / half_width
    weight = 1.0 / sigma

    def begin(r, carry):
        value = loads[r].astype(jnp.float32) / centre
        state[r] = value
        change[r] = value
        pad0[rows + r] = value.astype(jnp.bfloat16)
        return carry

    lax.fori_loop(0, rows, begin, 0)
    for copy in halo:
        copy.wait()

    def sides(r, carry):
        pad0[r] = (low[r].astype(jnp.float32) / centre).astype(jnp.bfloat16)
        pad0[2 * rows + r] = (high[r].astype(jnp.float32) / centre).astype(jnp.bfloat16)
        return carry

    lax.fori_loop(0, rows, sides, 0)

    for sweep in range(SWEEPS):
        pad = (pad0, pad1)[sweep]
        following = 1.0 / (2.0 * sigma - weight)
        keep = following * weight
        gain = 2.0 * following / half_width

        def row(r, carry, pad=pad, keep=keep, gain=gain, sweep=sweep):
            product = jnp.zeros(state.shape[1:], jnp.float32)
            for k in range(coarse.shape[1]):
                product += jnp.dot(
                    coarse[r, k], pad[cols[r, k]], preferred_element_type=jnp.float32
                )
            residual = loads[r].astype(jnp.float32) - product
            update = keep * change[r] + gain * residual
            value = state[r] + update
            if sweep + 1 < SWEEPS:
                change[r] = update
                state[r] = value
                pad1[rows + r] = value.astype(jnp.bfloat16)
            else:
                smoothed[r] = value.astype(jnp.bfloat16)
            return carry

        lax.fori_loop(0, rows, row, 0)
        weight = following
        if sweep + 1 < SWEEPS:
            own = pad1.at[pl.ds(rows, rows)]
            copies = [
                remote(own, pad1.at[pl.ds(0, rows)], hsend.at[2], hrecv.at[2], up),
                remote(own, pad1.at[pl.ds(2 * rows, rows)], hsend.at[3], hrecv.at[3], down),
            ]
            for copy in copies:
                copy.start()
            for copy in copies:
                copy.wait()
    for copy in first + second:
        copy.wait_send()


def coarse_and_smooth(n_gx, partial, packs, merges, cols, loads):
    _, pieces, width, _ = partial.shape
    rows, _, columns = loads.shape
    half = width // 2
    bf16, f32 = jnp.bfloat16, jnp.float32
    n_b = 2 * len(CHUNKS)
    peers = 6 + n_gx - 1
    spans = [k1 - k0 for k0, k1 in CHUNKS for _ in range(2)]
    bufs = [VMEM((3, LINE, n, half, width), bf16) for n in spans]
    bufs += [VMEM((4 * LINE + 1, n, half, width), bf16) for n in spans]
    bufs += [VMEM((4, rows, n, half, width), bf16) for n in spans]
    bufs += [VMEM((3, rows, n, half, width), bf16) for n in spans]
    vmem, smem = pl.BlockSpec(memory_space=VMEM), pl.BlockSpec(memory_space=SMEM)
    return pl.pallas_call(
        functools.partial(coarse_kernel, n_gx),
        out_shape=(
            jax.ShapeDtypeStruct((rows, pieces, width, width), bf16),
            jax.ShapeDtypeStruct((rows, width, columns), bf16),
        ),
        in_specs=[vmem, smem, smem, smem, vmem],
        out_specs=(vmem, vmem),
        scratch_shapes=[
            VMEM((rows, width, columns), bf16),
            VMEM((rows, width, columns), bf16),
            VMEM((3 * rows, width, columns), bf16),
            VMEM((3 * rows, width, columns), bf16),
            VMEM((rows, width, columns), f32),
            VMEM((rows, width, columns), f32),
            VMEM((4, 8, 128), f32),
            VMEM((peers, 8, 128), f32),
            DMA((n_b, 3)), DMA((n_b, 3)), DMA((n_b, 3)), DMA((n_b, 3)),
            DMA((4,)), DMA((4,)), DMA((peers,)), DMA((peers,)),
            *bufs,
        ],
        compiler_params=pltpu.CompilerParams(
            collective_id=2, has_side_effects=True, vmem_limit_bytes=58 << 20
        ),
    )(partial, packs, merges, cols, loads)


def per_device(n_gx, a_blocks, prolong, neighbour, ghost_send, fine_agg, balance, coarse_cols, loads):
    slots = balance.shape[2]
    table = jnp.concatenate(
        [
            jnp.pad(fine_agg, (0, 128 - fine_agg.shape[0]))[None],
            jnp.pad(balance[0, 0], (0, 128 - slots))[None],
            jnp.zeros((6, 128), jnp.int32),
        ]
    )
    ghosts, tables = exchange_ghosts(prolong, ghost_send[0, 0], table)
    packs, merges = make_tables(tables, slots, loads.shape[0])
    partial = products(a_blocks, prolong, ghosts, neighbour)
    device = lax.axis_index("gx") * NX * NZ + lax.axis_index("gy")
    near_cols = coarse_cols - (device - 1) * loads.shape[0]
    return coarse_and_smooth(n_gx, partial, packs, merges, near_cols, loads)


def solution(mesh):
    return jax.shard_map(
        functools.partial(per_device, mesh.shape["gx"]),
        mesh=mesh,
        in_specs=(
            P(("gx", "gy"), None, None, None),
            P(("gx", "gy"), None, None),
            P(("gx", "gy"), None),
            P("gx", "gy", None, None),
            P(("gx", "gy")),
            P("gx", "gy", None),
            P(("gx", "gy"), None),
            P(("gx", "gy"), None, None),
        ),
        out_specs=(P(("gx", "gy"), None, None, None), P(("gx", "gy"), None, None)),
        check_vma=False,
    )
```

time: 664 us -> 246 us (0.37)
  waiting for transfers between devices: 377 us -> 0 us
  Pallas kernels: 0 us -> 231 us
  blocking collectives: 91.2 us -> 0 us
  local copies, waits for them, and re-layouts: 80.3 us -> 11.9 us
  matrix products: 42.6 us -> 0 us
  starting transfers between devices: 42.6 us -> 0 us
  between operations: 16.5 us -> 0.69 us
  other arithmetic: 9.69 us -> 0.67 us
    pallas_call x0 -> x4, Pallas kernels: none -> 231 us  [the longest x1 152 us: coarse_and_smooth(): pl.pallas_call(functools.partial(coarse_kernel, n_gx), out_shape=(jax.Sha...]
    all_to_all x4 -> x0, waiting for transfers between devices: 229 us -> none  [the longest x1 188 us: per_device(): lax.all_to_all(buffer, 'gy', split_axis=0, concat_axis=0, tiled=True)]
    all_gather x1 -> x0, waiting for transfers between devices: 127 us -> none  [per_device(): lax.all_gather(prolong, 'gy', axis=0, tiled=True)]
    pmax x1 -> x0, blocking collectives: 71.5 us -> none  [per_device(): largest = lax.pmax(jnp.max(magnitude), ('gx', 'gy'))]
    dot_general x5 -> x0, matrix products: 42.6 us -> none  [the longest x1 18.1 us: per_device(): jnp.einsum('iac,ikad->ikcd', prolong, applied, preferred_element_type=jnp...]
    all_to_all x4 -> x0, starting transfers between devices: 34.6 us -> none  [the longest x1 12.6 us: per_device(): lax.all_to_all(moving_labels, 'gy', split_axis=0, concat_axis=0, tiled=True)]
    gather x4 -> x0, local copies, waits for them, and re-layouts: 26.4 us -> none  [the longest x1 11 us: per_device(): everyone[pool_index.reshape(-1)]]
    scatter x4 -> x0, local copies, waits for them, and re-layouts: 25.7 us -> none  [the longest x2 24.4 us: place_rows(): buffer = jnp.zeros((capacity,) + values.shape[1:], values.dtype).at[posit...]
  transfers between devices with their start and end apart: 9 -> 0, of which waited for: 7 -> 0; matrix products, arithmetic and copies ran while one was open for 17% -> 0% of each run, Pallas kernels for 0% -> 0%
where the time goes in v1:
time: 246 us; the launch traced here: 245 us
  Pallas kernels  231 us (94%)
  local copies, waits for them, and re-layouts  11.9 us (5%)
    pallas_call x1, Pallas kernels, coarse_and_smooth(): pl.pallas_call(functools.partial(coarse_kernel, n_gx), out_shape=(jax.Sha...  152 us
    pallas_call x1, Pallas kernels, exchange_ghosts(): pl.pallas_call(ghost_kernel, out_shape=(jax.ShapeDtypeStruct((peers * GCA...  43.7 us
    pallas_call x1, Pallas kernels, products(): pl.pallas_call(product_kernel, grid_spec=pltpu.PrefetchScalarGridSpec(num...  24.6 us
    pallas_call x1, Pallas kernels, make_tables(): pl.pallas_call(functools.partial(table_kernel, slots, coarse_rows), out_s...  11.6 us
    unnamed x15, local copies, waits for them, and re-layouts  10.4 us

profile of v1, /device:TPU:1, one launch (start us, length us, event | category | flops | bytes accessed | tf_op | source)
XLA Modules:
  0.0 244.8 jit_solution(8397638347490014184)
XLA Ops:
  0.6 0.7 pad_bitcast_fusion
  1.3 0.1 pad.12.clone
  1.4 0.1 add_add_fusion.table
  1.5 0.8 copy.12
  2.2 0.0 copy-start.1
  2.2 1.4 copy-done.1
  3.6 43.7 %shard_map.95 = (bf16[48,256,128]{2,1,0:T(8,128)(2,1)S(1)}, s32[4,4,8,128]{3,2,1,0:T(8,128)S(1)}) custom-call(bf16[24,256,128]{2,1,0:T(8,128)(2,1)S(1)} %copy-done.1, s32[16,3]{1,0:T(8,128)S(1)} %bitcast.6, s32[8,128]{1,0:T(8,128)S(1)} %add_add_fusion.table), custom_call_target="tpu_custom_call" | custom-call | tf_op jit(solution)/shard_map/pallas_call | solution.py:155
  47.3 0.0 copy-start.3
  47.3 0.6 copy-done.3
  48.0 11.6 %shard_map.97 = (s32[2,48]{1,0:T(2,128)}, s32[2,96]{1,0:T(2,128)}) custom-call(s32[4,4,8,128]{3,2,1,0:T(8,128)} %copy-done.3), custom_call_target="tpu_custom_call" | custom-call | tf_op jit(solution)/shard_map/pallas_call | solution.py:237
  59.6 0.8 copy.11.neighbour
  60.3 0.0 copy-start.2
  60.3 1.4 copy-done.2
  61.7 0.0 copy-start.5
  61.7 24.6 %shard_map.96.partial = bf16[24,7,128,128]{3,2,1,0:T(8,128)(2,1)S(1)} custom-call(s32[24,6]{1,0:T(8,128)S(1)} %copy.11.neighbour, bf16[24,7,256,256]{3,2,1,0:T(8,128)(2,1)} %blocks.1, bf16[24,256,128]{2,1,0:T(8,128)(2,1)S(1)} %copy-done.2, bf16[48,256,128]{2,1,0:T(8,128)(2,1)S(1)} %get-tuple-element.6.ghosts), custom_call_target="tpu_custom_call" | custom-call | flops 4227858432 | bytes 22020096 | tf_op jit(solution)/shard_map/pallas_call | solution.py:282
  86.4 0.0 copy-start
  86.4 2.4 copy-done
  88.8 0.0 copy-done.5
  88.8 0.6 broadcast_subtract_fusion.cols
  89.4 151.5 %shard_map.98 = (bf16[8,7,128,128]{3,2,1,0:T(8,128)(2,1)}, bf16[8,128,256]{2,1,0:T(8,128)(2,1)}) custom-call(bf16[24,7,128,128]{3,2,1,0:T(8,128)(2,1)} %copy-done, s32[2,48]{1,0:T(2,128)} %get-tuple-element.8.packs, s32[2,96]{1,0:T(2,128)} %get-tuple-element.9.merges, s32[8,7]{1,0:T(8,128)} %broadcast_subtract_fusion.cols, bf16[8,128,256]{2,1,0:T(8,128)(2,1)} %loads.1), custom_call_target="tpu_custom_call" | custom-call | tf_op jit(solution)/shard_map/pallas_call | solution.py:516
  241.0 0.0 copy-start.4
  241.0 3.0 %copy.15 = bf16[8,7,128,128]{3,2,1,0:T(8,128)(2,1)} copy(bf16[8,7,128,128]{3,2,1,0:T(8,128)(2,1)} %get-tuple-element.14) | data formatting | bytes 3670016
  244.0 0.0 copy-done.4
  244.0 0.8 copy.16
  (1 shorter events, 0.0 us)
Async XLA Ops:
  2.2 1.4 copy-start.1
  47.3 0.6 copy-start.3
  60.3 1.4 copy-start.2
  61.7 27.1 %copy-start.5 = (s32[8,7]{1,0:T(8,128)S(1)}, s32[8,7]{1,0:T(8,128)}, u32[]{:S(2)}) copy-start(s32[8,7]{1,0:T(8,128)} %param.14) | copy-start | bytes 676
  86.4 2.4 copy-start
  241.0 3.0 %copy-start.4 = (bf16[8,128,256]{2,1,0:T(8,128)(2,1)S(1)}, bf16[8,128,256]{2,1,0:T(8,128)(2,1)}, u32[]{:S(2)}) copy-start(bf16[8,128,256]{2,1,0:T(8,128)(2,1)} %get-tuple-element.15) | copy-start | bytes 1572868

commit v2 on v0

v2 whole, which is shorter than its diff:
```python
import functools

import jax
import jax.numpy as jnp
from jax import lax
from jax.experimental import pallas as pl
from jax.experimental.pallas import tpu as pltpu
from jax.sharding import PartitionSpec as P

MESH = pl.DeviceIdType.MESH
NX = 4
NZ = 4
GCAP = 3
LINE = 12
SWEEPS = 2
CHUNKS = ((0, 1), (1, 2), (2, 4), (4, 6), (6, 7))
SPAN = max(k1 - k0 for k0, k1 in CHUNKS)
AHEAD = 8
TABLE = 24
VMEM = pltpu.VMEM
SMEM = pltpu.SMEM
DMA = pltpu.SemaphoreType.DMA


def place():
    me = lax.axis_index("gy")
    return lax.axis_index("gx"), lax.div(me, NZ), lax.rem(me, NZ)


def line_peer(axis, step):
    gx, x, z = place()
    if axis == 0:
        return gx, lax.rem(x + step, NX) * NZ + z
    return gx, x * NZ + lax.rem(z + step, NZ)


def greet(peers):
    barrier = pltpu.get_barrier_semaphore()
    for peer in peers:
        pl.semaphore_signal(barrier, 1, device_id=peer, device_id_type=MESH)
    pl.semaphore_wait(barrier, len(peers))


def remote(src, dst, send, recv, peer):
    return pltpu.make_async_remote_copy(
        src_ref=src, dst_ref=dst, send_sem=send, recv_sem=recv, device_id=peer, device_id_type=MESH
    )


def parts_of(width):
    cut = width // 2
    return ((0, cut), (cut, width))


def index_tables(tables, coarse_rows, coords):
    shape = (128, 128)
    lane, sub = (lax.broadcasted_iota(jnp.int32, shape, d) for d in (1, 0))
    bits = coarse_rows.bit_length() - 1

    def quarter(n):
        return sum((n >= 24 * q).astype(jnp.int32) for q in (1, 2, 3))

    def down(row):
        return jnp.transpose(jnp.broadcast_to(row, shape))

    def total(mask, values=None):
        picked = mask.astype(jnp.int32) if values is None else jnp.where(mask, values, 0)
        return jnp.sum(picked, axis=0, keepdims=True)

    lane_row = lane[0:1]
    source, source_down = quarter(lane), quarter(sub)
    source_row = source[0:1]
    packs, merges = [], []
    for axis in (0, 1):
        label = jnp.zeros((1, 128), jnp.int32)
        for s in range(4):
            entry = tables[s, coords[1], 16:24, :] if axis == 0 else tables[coords[0], s, 16:24, :]
            label += entry[axis : axis + 1]
        found = jnp.zeros((16, 128), jnp.int32)
        for owner in range(NX * NZ):
            slot_of = owner * 16 + lax.broadcasted_iota(jnp.int32, (16, 128), 0)
            found += jnp.where(slot_of == label, tables[owner // NZ, owner % NZ, 0:16, :], 0)
        target = jnp.sum(found, axis=0, keepdims=True)
        device = lax.shift_right_logical(target, bits)
        row = target & (coarse_rows - 1)
        sides = (lax.shift_right_logical(device, 2), device & 3)
        near, far = sides[axis], sides[1 - axis]
        before = sub < lane
        rank = total((down(near) == near) & (source_down == source) & before)
        used = (lane_row < 96) & (rank < LINE)
        mine = used & (near == coords[axis])
        goal = jnp.where(mine, far * coarse_rows + row, -1 - lane_row)
        order = total((down(goal) == goal) & before)
        key = down(jnp.where(mine & (order < 3), goal * 3 + order, -1))
        slot = down(source_row * LINE + rank)
        hit = key == lane
        merges.append(jnp.where(total(hit) > 0, total(hit, slot), 4 * LINE))
        own = down(jnp.where(used & (source_row == coords[axis]), near * LINE + rank, -1))
        packs.append(total(own == lane, sub - 24 * source_down))
    return jnp.concatenate(packs + merges + [jnp.zeros((4, 128), jnp.int32)])


def kernel(
    n_gx, blocks, prolong, ints, loads, coarse, smoothed,
    numbers, tables, slots_v, slots, packed, held, ghosts, arrived, partial,
    low, high, pad0, pad1, state, change, rowsum, peak, peaks,
    near_sem, block_sem, tsend1, trecv1, tsend2, trecv2, gsend1, grecv1, gsend2, grecv2, keep_sem,
    send1, recv1, send2, recv2, send3, recv3, send4, recv4, hsend, hrecv, psend, precv, *bufs,
):
    gx, x, z = place()
    gy = x * NZ + z
    coords = (x, z)
    count = NX * NZ
    fine_rows, order, width = prolong.shape
    rows = loads.shape[0]
    hrows = rows // 2
    half = order // 2
    cuts = parts_of(width)
    n_b = 2 * len(CHUNKS)
    out, pool, sums, passing, back = (bufs[n_b * n : n_b * (n + 1)] for n in range(5))
    up = (gx, lax.rem(gy + 1, count))
    down = (gx, lax.rem(gy + count - 1, count))
    across = [(lax.rem(gx + step, n_gx), gy) for step in range(1, n_gx)]
    lines = [line_peer(axis, step) for axis in (0, 1) for step in (1, 2, 3)]
    sent = []

    def go(copy):
        copy.start()
        sent.append(copy)

    def block_copy(c, i, slot):
        k0, k1 = CHUNKS[c]
        return pltpu.make_async_copy(
            blocks.at[i, pl.ds(k0, k1 - k0)], arrived.at[slot, pl.ds(0, k1 - k0)], block_sem.at[slot]
        )

    def fetch(c):
        for n in range(AHEAD):
            block_copy(c, n, n).start()

    own_numbers = pltpu.make_async_copy(ints.at[pl.ds(TABLE, numbers.shape[0])], numbers, near_sem.at[0])
    own_numbers.start()
    own_blocks = pltpu.make_async_copy(prolong, ghosts.at[pl.ds(0, fine_rows)], near_sem.at[1])
    own_blocks.start()
    table = ints.at[pl.ds(0, TABLE)]
    own_table = pltpu.make_async_copy(table, tables.at[x, z], near_sem.at[2])
    own_table.start()
    fetch(0)
    greet(lines + [up, down] + across)

    first_tables = [
        remote(table, tables.at[x, z], tsend1.at[s - 1], trecv1.at[s - 1], line_peer(0, s)) for s in (1, 2, 3)
    ]
    for copy in first_tables:
        go(copy)
    own_numbers.wait()

    for step in (2, 1, 3, 0):
        for axis in (0, 1):
            near = lax.rem(coords[axis] + step, 4)

            def pack_ghosts(n, carry, axis=axis, step=step, near=near):
                far, c = lax.div(n, GCAP), lax.rem(n, GCAP)
                peer = near * NZ + far if axis == 0 else far * NZ + near
                packed[axis, step, n] = prolong[numbers[peer, c], axis * half : (axis + 1) * half, :]
                return carry

            lax.fori_loop(0, 4 * GCAP, pack_ghosts, 0)
            if step:
                go(remote(
                    packed.at[axis, step], held.at[axis, step - 1],
                    gsend1.at[axis, step - 1], grecv1.at[axis, step - 1], line_peer(axis, step),
                ))

    own_table.wait()
    table_in = []
    for behind in (0, 1, 2, 3):
        if behind:
            first_tables[behind - 1].wait_recv()
        px = lax.rem(x + 4 - behind, 4)
        for s in (1, 2, 3):
            go(remote(
                tables.at[px, z], tables.at[px, z], tsend2.at[behind, s - 1], trecv2.at[behind, s - 1], line_peer(1, s)
            ))
            at = tables.at[px, lax.rem(z + 4 - s, 4)]
            table_in.append(remote(at, at, tsend2.at[behind, s - 1], trecv2.at[behind, s - 1], line_peer(1, s)))

    def ghost_rows(axis, px, pz):
        return ghosts.at[pl.ds(fine_rows + (px * NZ + pz) * GCAP, GCAP), pl.ds(axis * half, half), :]

    kept = []

    def forward_ghosts(behind, axis):
        if behind:
            remote(
                packed.at[axis, behind], held.at[axis, behind - 1],
                gsend1.at[axis, behind - 1], grecv1.at[axis, behind - 1], line_peer(axis, behind),
            ).wait_recv()
        at = held.at[axis, behind - 1] if behind else packed.at[axis, 0]
        near = lax.rem(coords[axis] + 4 - behind, 4)
        px, pz = (near, z) if axis == 0 else (x, near)
        for s in (1, 2, 3):
            far = lax.rem(coords[1 - axis] + s, 4)
            go(remote(
                at.at[pl.ds(far * GCAP, GCAP)], ghost_rows(axis, px, pz),
                gsend2.at[axis, behind, s - 1], grecv2.at[axis, behind, s - 1], line_peer(1 - axis, s),
            ))
        copy = pltpu.make_async_copy(
            at.at[pl.ds(coords[1 - axis] * GCAP, GCAP)], ghost_rows(axis, px, pz), keep_sem.at[axis, behind]
        )
        copy.start()
        kept.append(copy)

    def wait_ghosts():
        for axis in (0, 1):
            for behind in (0, 1, 2, 3):
                for s in (1, 2, 3):
                    near = lax.rem(coords[axis] + 4 - behind, 4)
                    far = lax.rem(coords[1 - axis] + 4 - s, 4)
                    at = ghost_rows(axis, near, far) if axis == 0 else ghost_rows(axis, far, near)
                    remote(
                        at, at, gsend2.at[axis, behind, s - 1], grecv2.at[axis, behind, s - 1], line_peer(1 - axis, s)
                    ).wait_recv()
        for copy in kept:
            copy.wait()
        own_blocks.wait()

    def multiply(c):
        k0, k1 = CHUNKS[c]

        def one_row(i, carry):
            slot = lax.rem(i, AHEAD)
            block_copy(c, i, slot).wait()
            applied = []
            for k in range(k0, k1):
                right = prolong[i] if k == 0 else ghosts[numbers[16 + i, k - 1]]
                applied.append(
                    jnp.dot(arrived[slot, k - k0], right, preferred_element_type=jnp.float32).astype(jnp.bfloat16)
                )
            value = lax.dot_general(
                prolong[i], jnp.concatenate(applied, axis=1), (((0,), (0,)), ((), ())),
                preferred_element_type=jnp.float32,
            ).astype(jnp.bfloat16)
            for k in range(k1 - k0):
                partial[i, k] = value[:, k * width : (k + 1) * width]

            @pl.when(i + AHEAD < fine_rows)
            def _():
                block_copy(c, i + AHEAD, slot).start()

            return carry

        lax.fori_loop(0, fine_rows, one_row, 0)
        if c + 1 < len(CHUNKS):
            fetch(c + 1)

    def scatter(c):
        span = CHUNKS[c][1] - CHUNKS[c][0]
        for step in (2, 1, 3, 0):
            for axis in (0, 1):
                b = 2 * c + axis
                near = lax.rem(coords[axis] + step, 4)

                def pack(n, carry, axis=axis, step=step, near=near, b=b):
                    value = partial[slots[axis, near * LINE + n], 0:span, cuts[axis][0] : cuts[axis][1], :]
                    if step:
                        out[b][step - 1, n] = value
                    else:
                        pool[b][near * LINE + n] = value
                    return carry

                lax.fori_loop(0, LINE, pack, 0)
                if step:
                    go(remote(
                        out[b].at[step - 1], pool[b].at[pl.ds(coords[axis] * LINE, LINE)],
                        send1.at[b, step - 1], recv1.at[b, step - 1], line_peer(axis, step),
                    ))
                else:
                    pool[b][4 * LINE] = jnp.zeros(pool[b].shape[1:], pool[b].dtype)

    def add_up(c):
        span = CHUNKS[c][1] - CHUNKS[c][0]
        for axis in (0, 1):
            b = 2 * c + axis
            for step in (1, 2, 3):
                source = lax.rem(coords[axis] + 4 - step, 4)
                remote(
                    out[b].at[step - 1], pool[b].at[pl.ds(source * LINE, LINE)],
                    send1.at[b, step - 1], recv1.at[b, step - 1], line_peer(axis, step),
                ).wait_recv()
            for step in (2, 1, 3, 0):
                far = lax.rem(coords[1 - axis] + step, 4)

                def merge(r, carry, axis=axis, b=b, step=step, far=far):
                    at = (far * rows + r) * 3
                    terms = [slots[2 + axis, at + n] for n in range(3)]
                    for k in range(span):
                        total = pool[b][terms[0], k].astype(jnp.float32)
                        total += pool[b][terms[1], k].astype(jnp.float32)
                        total += pool[b][terms[2], k].astype(jnp.float32)
                        sums[b][step, r, k] = total.astype(jnp.bfloat16)
                    return carry

                lax.fori_loop(0, rows, merge, 0)
                if step == 2:
                    for n, s in enumerate((1, 3)):
                        go(remote(
                            sums[b].at[2, pl.ds(n * hrows, hrows)], passing[b].at[n],
                            send2.at[b, n], recv2.at[b, n], line_peer(1 - axis, s),
                        ))
                elif step:
                    n = 0 if step == 1 else 1
                    part = pl.ds((1 - n) * hrows, hrows)
                    go(remote(
                        sums[b].at[step, part], back[b].at[n, part],
                        send3.at[b, n], recv3.at[b, n], line_peer(1 - axis, step),
                    ))

    def relay(c):
        span = CHUNKS[c][1] - CHUNKS[c][0]
        for axis in (0, 1):
            b = 2 * c + axis
            for n, step in enumerate((1, 3)):
                remote(
                    sums[b].at[2, pl.ds(n * hrows, hrows)], passing[b].at[n],
                    send2.at[b, n], recv2.at[b, n], line_peer(1 - axis, step),
                ).wait_recv()

                def take(r, carry, b=b, n=n, step=step):
                    for k in range(span):
                        total = sums[b][step, n * hrows + r, k].astype(jnp.float32)
                        total += passing[b][n, r, k].astype(jnp.float32)
                        sums[b][step, n * hrows + r, k] = total.astype(jnp.bfloat16)
                    return carry

                lax.fori_loop(0, hrows, take, 0)
                part = pl.ds(n * hrows, hrows)
                go(remote(
                    sums[b].at[step, part], back[b].at[n, part],
                    send4.at[b, n], recv4.at[b, n], line_peer(1 - axis, step),
                ))

    def finish(c):
        k0, k1 = CHUNKS[c]
        for axis in (0, 1):
            b = 2 * c + axis
            lo, hi = cuts[axis]
            for n, step in enumerate((1, 3)):
                for m, (send, recv) in enumerate(((send3, recv3), (send4, recv4))):
                    part = pl.ds((1 - n if m == 0 else n) * hrows, hrows)
                    remote(
                        sums[b].at[step, part], back[b].at[n, part],
                        send.at[b, n], recv.at[b, n], line_peer(1 - axis, step),
                    ).wait_recv()

            def settle(r, carry, b=b, lo=lo, hi=hi):
                size = jnp.zeros((hi - lo, width), jnp.float32)
                for k in range(k1 - k0):
                    total = sums[b][0, r, k].astype(jnp.float32)
                    total += back[b][0, r, k].astype(jnp.float32)
                    total += back[b][1, r, k].astype(jnp.float32)
                    rounded = total.astype(jnp.bfloat16)
                    coarse[r, k0 + k, lo:hi, :] = rounded
                    size += jnp.abs(rounded.astype(jnp.float32))
                rowsum[r, lo:hi, :] = size if c == 0 else rowsum[r, lo:hi, :] + size
                return carry

            lax.fori_loop(0, rows, settle, 0)

    multiply(0)
    for copy in table_in:
        copy.wait_recv()
    slots_v[...] = index_tables(tables, rows, coords)
    forward_ghosts(0, 0)
    forward_ghosts(0, 1)
    slot_copy = pltpu.make_async_copy(slots_v, slots, near_sem.at[3])
    slot_copy.start()
    slot_copy.wait()
    for behind in (1, 3, 2):
        for axis in (0, 1):
            forward_ghosts(behind, axis)
    scatter(0)
    wait_ghosts()
    for c in range(1, len(CHUNKS)):
        multiply(c)
        scatter(c)
        if c == 1:
            add_up(0)
        elif c == 2:
            relay(0)
    halo = [
        remote(loads, low, hsend.at[0], hrecv.at[0], up),
        remote(loads, high, hsend.at[1], hrecv.at[1], down),
    ]
    for copy in halo:
        copy.start()
    for c in range(1, len(CHUNKS)):
        add_up(c)
        if c > 1:
            relay(c - 1)
            finish(c - 2)
    relay(len(CHUNKS) - 1)
    finish(len(CHUNKS) - 2)
    finish(len(CHUNKS) - 1)

    def row_peak(r, top):
        return jnp.maximum(top, jnp.sum(rowsum[r], axis=1, keepdims=True))

    top = lax.fori_loop(0, rows, row_peak, jnp.zeros((width, 1), jnp.float32))
    peak[0] = jnp.broadcast_to(jnp.max(top, axis=0, keepdims=True), peak.shape[1:])

    base = 0
    for stage, peers in enumerate((lines[:3], lines[3:], across)):
        copies = []
        for n, peer in enumerate(peers):
            copy = remote(peak.at[stage], peaks.at[base + n], psend.at[base + n], precv.at[base + n], peer)
            copy.start()
            copies.append(copy)
        for copy in copies:
            copy.wait()
        top = peak[stage]
        for n in range(len(peers)):
            top = jnp.maximum(top, peaks[base + n])
        peak[stage + 1] = top
        base += len(peers)

    largest = peak[3, 0:1, 0:1]
    lower_end = largest / 30.0
    centre = (largest + lower_end) / 2.0
    half_width = (largest - lower_end) / 2.0
    sigma = centre / half_width
    weight = 1.0 / sigma

    def begin(r, carry):
        value = loads[r].astype(jnp.float32) / centre
        state[r] = value
        change[r] = value
        pad0[rows + r] = value.astype(jnp.bfloat16)
        return carry

    lax.fori_loop(0, rows, begin, 0)
    for copy in halo:
        copy.wait()

    def sides(r, carry):
        pad0[r] = (low[r].astype(jnp.float32) / centre).astype(jnp.bfloat16)
        pad0[2 * rows + r] = (high[r].astype(jnp.float32) / centre).astype(jnp.bfloat16)
        return carry

    lax.fori_loop(0, rows, sides, 0)

    for sweep in range(SWEEPS):
        pad = (pad0, pad1)[sweep]
        following = 1.0 / (2.0 * sigma - weight)
        keep = following * weight
        gain = 2.0 * following / half_width

        def row(r, carry, pad=pad, keep=keep, gain=gain, sweep=sweep):
            product = jnp.zeros(state.shape[1:], jnp.float32)
            for k in range(coarse.shape[1]):
                product += jnp.dot(
                    coarse[r, k], pad[numbers[40 + r, k]], preferred_element_type=jnp.float32
                )
            residual = loads[r].astype(jnp.float32) - product
            update = keep * change[r] + gain * residual
            value = state[r] + update
            if sweep + 1 < SWEEPS:
                change[r] = update
                state[r] = value
                pad1[rows + r] = value.astype(jnp.bfloat16)
            else:
                smoothed[r] = value.astype(jnp.bfloat16)
            return carry

        lax.fori_loop(0, rows, row, 0)
        weight = following
        if sweep + 1 < SWEEPS:
            own = pad1.at[pl.ds(rows, rows)]
            copies = [
                remote(own, pad1.at[pl.ds(0, rows)], hsend.at[2], hrecv.at[2], up),
                remote(own, pad1.at[pl.ds(2 * rows, rows)], hsend.at[3], hrecv.at[3], down),
            ]
            for copy in copies:
                copy.start()
            for copy in copies:
                copy.wait()
    for copy in sent:
        copy.wait_send()


def per_device(n_gx, a_blocks, prolong, neighbour, ghost_send, fine_agg, balance, coarse_cols, loads):
    fine_rows, pieces, order, _ = a_blocks.shape
    width = prolong.shape[2]
    rows, _, columns = loads.shape
    count = NX * NZ
    me = lax.axis_index("gy")
    device = lax.axis_index("gx") * count + me
    near_cols = coarse_cols - (device - 1) * rows
    lane = jnp.arange(128, dtype=jnp.int32)
    fourfold = jnp.pad(jnp.concatenate([fine_agg] * 4), (0, 128 - 4 * fine_rows))
    labels = [
        jnp.where((lane >= at * fine_rows) & (lane < (at + 1) * fine_rows), fourfold, 0)[None]
        for at in (me // NZ, me % NZ)
    ]

    def wide(values):
        return jnp.pad(values, ((0, 0), (0, 128 - values.shape[1])))

    ints = jnp.concatenate(
        [
            jnp.broadcast_to(balance[0, 0][:, None], (count, 128)),
            *labels,
            jnp.zeros((6, 128), jnp.int32),
            wide(ghost_send[0, 0]),
            wide(neighbour),
            wide(near_cols),
        ]
    )
    bf16, f32 = jnp.bfloat16, jnp.float32
    n_b = 2 * len(CHUNKS)
    peers = 6 + n_gx - 1
    shapes = [(k1 - k0, hi - lo, width) for k0, k1 in CHUNKS for lo, hi in parts_of(width)]
    bufs = [VMEM((3, LINE, *n), bf16) for n in shapes]
    bufs += [VMEM((4 * LINE + 1, *n), bf16) for n in shapes]
    bufs += [VMEM((4, rows, *n), bf16) for n in shapes]
    bufs += [VMEM((2, rows // 2, *n), bf16) for n in shapes]
    bufs += [VMEM((2, rows, *n), bf16) for n in shapes]
    vmem = pl.BlockSpec(memory_space=VMEM)
    return pl.pallas_call(
        functools.partial(kernel, n_gx),
        out_shape=(
            jax.ShapeDtypeStruct((rows, pieces, width, width), bf16),
            jax.ShapeDtypeStruct((rows, width, columns), bf16),
        ),
        in_specs=[pl.BlockSpec(memory_space=pl.ANY), vmem, vmem, vmem],
        out_specs=(vmem, vmem),
        scratch_shapes=[
            SMEM((ints.shape[0] - TABLE, 128), jnp.int32),
            VMEM((NX, NZ, TABLE, 128), jnp.int32),
            VMEM((8, 128), jnp.int32),
            SMEM((8, 128), jnp.int32),
            VMEM((2, 4, 4 * GCAP, order // 2, width), bf16),
            VMEM((2, 3, 4 * GCAP, order // 2, width), bf16),
            VMEM((fine_rows + count * GCAP, order, width), bf16),
            VMEM((AHEAD, SPAN, order, order), bf16),
            VMEM((fine_rows, SPAN, width, width), bf16),
            VMEM((rows, width, columns), bf16),
            VMEM((rows, width, columns), bf16),
            VMEM((3 * rows, width, columns), bf16),
            VMEM((3 * rows, width, columns), bf16),
            VMEM((rows, width, columns), f32),
            VMEM((rows, width, columns), f32),
            VMEM((rows, width, width), f32),
            VMEM((4, 8, 128), f32),
            VMEM((peers, 8, 128), f32),
            DMA((4,)), DMA((AHEAD,)),
            DMA((3,)), DMA((3,)), DMA((4, 3)), DMA((4, 3)),
            DMA((2, 3)), DMA((2, 3)), DMA((2, 4, 3)), DMA((2, 4, 3)), DMA((2, 4)),
            DMA((n_b, 3)), DMA((n_b, 3)),
            *[DMA((n_b, 2)) for _ in range(6)],
            DMA((4,)), DMA((4,)), DMA((peers,)), DMA((peers,)),
            *bufs,
        ],
        compiler_params=pltpu.CompilerParams(
            collective_id=1, has_side_effects=True, vmem_limit_bytes=60 << 20
        ),
        cost_estimate=pl.CostEstimate(
            flops=2 * fine_rows * pieces * order * width * (order + width),
            bytes_accessed=2 * fine_rows * pieces * order * order,
            transcendentals=0,
        ),
    )(a_blocks, prolong, ints, loads)


def solution(mesh):
    return jax.shard_map(
        functools.partial(per_device, mesh.shape["gx"]),
        mesh=mesh,
        in_specs=(
            P(("gx", "gy"), None, None, None),
            P(("gx", "gy"), None, None),
            P(("gx", "gy"), None),
            P("gx", "gy", None, None),
            P(("gx", "gy")),
            P("gx", "gy", None),
            P(("gx", "gy"), None),
            P(("gx", "gy"), None, None),
        ),
        out_specs=(P(("gx", "gy"), None, None, None), P(("gx", "gy"), None, None)),
        check_vma=False,
    )
```

time: 664 us -> 202 us (0.30)
  waiting for transfers between devices: 377 us -> 0 us
  Pallas kernels: 0 us -> 191 us
  blocking collectives: 91.2 us -> 0 us
  local copies, waits for them, and re-layouts: 80.3 us -> 9.06 us
  matrix products: 42.6 us -> 0 us
  starting transfers between devices: 42.6 us -> 0 us
  between operations: 16.5 us -> 0.68 us
  other arithmetic: 9.69 us -> 1.58 us
    all_to_all x4 -> x0, waiting for transfers between devices: 229 us -> none  [the longest x1 188 us: per_device(): lax.all_to_all(buffer, 'gy', split_axis=0, concat_axis=0, tiled=True)]
    pallas_call x0 -> x1, Pallas kernels: none -> 191 us  [per_device(): pl.pallas_call(functools.partial(kernel, n_gx), out_shape=(jax.ShapeDtype...]
    all_gather x1 -> x0, waiting for transfers between devices: 127 us -> none  [per_device(): lax.all_gather(prolong, 'gy', axis=0, tiled=True)]
    pmax x1 -> x0, blocking collectives: 71.5 us -> none  [per_device(): largest = lax.pmax(jnp.max(magnitude), ('gx', 'gy'))]
    dot_general x5 -> x0, matrix products: 42.6 us -> none  [the longest x1 18.1 us: per_device(): jnp.einsum('iac,ikad->ikcd', prolong, applied, preferred_element_type=jnp...]
    all_to_all x4 -> x0, starting transfers between devices: 34.6 us -> none  [the longest x1 12.6 us: per_device(): lax.all_to_all(moving_labels, 'gy', split_axis=0, concat_axis=0, tiled=True)]
    gather x4 -> x0, local copies, waits for them, and re-layouts: 26.4 us -> none  [the longest x1 11 us: per_device(): everyone[pool_index.reshape(-1)]]
    scatter x4 -> x0, local copies, waits for them, and re-layouts: 25.7 us -> none  [the longest x2 24.4 us: place_rows(): buffer = jnp.zeros((capacity,) + values.shape[1:], values.dtype).at[posit...]
  transfers between devices with their start and end apart: 9 -> 0, of which waited for: 7 -> 0; matrix products, arithmetic and copies ran while one was open for 17% -> 0% of each run, Pallas kernels for 0% -> 0%
where the time goes in v2:
time: 202 us
  Pallas kernels  191 us (95%)
  local copies, waits for them, and re-layouts  9.06 us (4%)
    pallas_call x1, Pallas kernels, per_device(): pl.pallas_call(functools.partial(kernel, n_gx), out_shape=(jax.ShapeDtype...  191 us
    unnamed x5, local copies, waits for them, and re-layouts  4.56 us

profile of v2, /device:TPU:1, one launch (start us, length us, event | category | flops | bytes accessed | tf_op | source)
XLA Modules:
  0.0 202.1 jit_solution(3468686035971657821)
XLA Ops:
  0.7 0.9 pad_add_fusion
  1.5 0.7 broadcast_subtract_fusion
  2.2 0.8 copy.12
  3.0 0.7 broadcast_in_dim.22
  3.7 0.8 copy.11
  4.5 3.0 %concatenate.7.ints = s32[72,128]{1,0:T(8,128)} concatenate(s32[16,128]{1,0:T(8,128)S(1)} %broadcast_in_dim.22, s32[1,128]{1,0:T(1,128)S(1)} %get-tuple-element.3, s32[1,128]{1,0:T(1,128)S(1)} %get-tuple-element.2, s32[6,128]{1,0:T(8,128)S(1)} %broadcast_in_dim.26, s32[16,128]{1,0:T(8,128)S(1)} %pad.17, s32[24,128]{1,0:T(8,128)S(1)} %pad.18, s32[8,128]{1,0:T(8,128)S(1)} %pad.19), dimensions={0} | concatenate | bytes 73728 | tf_op jit(solution)/shard_map/concatenate | solution.py:509
  7.5 190.8 %shard_map.95 = (bf16[8,7,128,128]{3,2,1,0:T(8,128)(2,1)}, bf16[8,128,256]{2,1,0:T(8,128)(2,1)}) custom-call(bf16[24,7,256,256]{3,2,1,0:T(8,128)(2,1)} %blocks.1, bf16[24,256,128]{2,1,0:T(8,128)(2,1)} %prolong.1, s32[72,128]{1,0:T(8,128)} %concatenate.7.ints, bf16[8,128,256]{2,1,0:T(8,128)(2,1)} %loads.1), custom_call_target="tpu_custom_call" | custom-call | flops 4227858432 | bytes 22020096 | tf_op jit(solution)/shard_map/pallas_call | solution.py:529
  198.3 0.0 copy-start
  198.3 3.0 %copy.15 = bf16[8,7,128,128]{3,2,1,0:T(8,128)(2,1)} copy(bf16[8,7,128,128]{3,2,1,0:T(8,128)(2,1)} %get-tuple-element.6) | data formatting | bytes 3670016
  201.3 0.0 copy-done
  201.3 0.8 copy.16
  (5 shorter events, 0.0 us)
Async XLA Ops:
  198.3 3.0 %copy-start = (bf16[8,128,256]{2,1,0:T(8,128)(2,1)S(1)}, bf16[8,128,256]{2,1,0:T(8,128)(2,1)}, u32[]{:S(2)}) copy-start(bf16[8,128,256]{2,1,0:T(8,128)(2,1)} %get-tuple-element.7) | copy-start | bytes 1572868

commit v3 on v2

--- a/solution.py
+++ b/solution.py
@@ -12,11 +12,10 @@
 NZ = 4
 GCAP = 3
 LINE = 12
-SWEEPS = 2
 CHUNKS = ((0, 1), (1, 2), (2, 4), (4, 6), (6, 7))
 SPAN = max(k1 - k0 for k0, k1 in CHUNKS)
 AHEAD = 8
-TABLE = 24
+SCALE = 1.0 / 256.0
 VMEM = pltpu.VMEM
 SMEM = pltpu.SMEM
 DMA = pltpu.SemaphoreType.DMA
@@ -74,12 +73,13 @@
     for axis in (0, 1):
         label = jnp.zeros((1, 128), jnp.int32)
         for s in range(4):
-            entry = tables[s, coords[1], 16:24, :] if axis == 0 else tables[coords[0], s, 16:24, :]
-            label += entry[axis : axis + 1]
+            entry = tables[s, coords[1], 0:1, :] if axis == 0 else tables[coords[0], s, 0:1, :]
+            label += pltpu.roll(entry, 24 * s, 1) if s else entry
         found = jnp.zeros((16, 128), jnp.int32)
         for owner in range(NX * NZ):
             slot_of = owner * 16 + lax.broadcasted_iota(jnp.int32, (16, 128), 0)
-            found += jnp.where(slot_of == label, tables[owner // NZ, owner % NZ, 0:16, :], 0)
+            given = down(tables[owner // NZ, owner % NZ, 1:2, :])[0:16]
+            found += jnp.where(slot_of == label, given, 0)
         target = jnp.sum(found, axis=0, keepdims=True)
         device = lax.shift_right_logical(target, bits)
         row = target & (coarse_rows - 1)
@@ -101,9 +101,9 @@
 
 
 def kernel(
-    n_gx, blocks, prolong, ints, loads, coarse, smoothed,
-    numbers, tables, slots_v, slots, packed, held, ghosts, arrived, partial,
-    low, high, pad0, pad1, state, change, rowsum, peak, peaks,
+    n_gx, blocks, prolong, neighbours, sends, labels, balance, columns, loads, coarse, smoothed,
+    near, wanted, cols, table, tables, slots_v, slots, packed, held, ghosts, arrived, partial,
+    pad0, pad1, product, product_out, product_in, state, change, rowsum, peak, peaks,
     near_sem, block_sem, tsend1, trecv1, tsend2, trecv2, gsend1, grecv1, gsend2, grecv2, keep_sem,
     send1, recv1, send2, recv2, send3, recv3, send4, recv4, hsend, hrecv, psend, precv, *bufs,
 ):
@@ -138,14 +138,27 @@
         for n in range(AHEAD):
             block_copy(c, n, n).start()
 
-    own_numbers = pltpu.make_async_copy(ints.at[pl.ds(TABLE, numbers.shape[0])], numbers, near_sem.at[0])
-    own_numbers.start()
+    own_numbers = [
+        pltpu.make_async_copy(source, held_in, near_sem.at[4 + n])
+        for n, (source, held_in) in enumerate(((sends, wanted), (neighbours, near), (columns, cols)))
+    ]
+    for copy in own_numbers:
+        copy.start()
     own_blocks = pltpu.make_async_copy(prolong, ghosts.at[pl.ds(0, fine_rows)], near_sem.at[1])
     own_blocks.start()
-    table = ints.at[pl.ds(0, TABLE)]
+    table[...] = jnp.zeros(table.shape, jnp.int32)
+    table[0:1, 0:fine_rows] = labels[...]
+    table[1:2, 0 : balance.shape[1]] = balance[...]
     own_table = pltpu.make_async_copy(table, tables.at[x, z], near_sem.at[2])
     own_table.start()
     fetch(0)
+
+    def scale_row(r, carry):
+        pad0[rows + r] = (loads[r].astype(jnp.float32) * SCALE).astype(jnp.bfloat16)
+        product[r] = jnp.zeros(product.shape[1:], jnp.float32)
+        return carry
+
+    lax.fori_loop(0, rows, scale_row, 0)
     greet(lines + [up, down] + across)
 
     first_tables = [
@@ -153,16 +166,17 @@
     ]
     for copy in first_tables:
         go(copy)
-    own_numbers.wait()
+    for copy in own_numbers:
+        copy.wait()
 
     for step in (2, 1, 3, 0):
         for axis in (0, 1):
-            near = lax.rem(coords[axis] + step, 4)
-
-            def pack_ghosts(n, carry, axis=axis, step=step, near=near):
+            side = lax.rem(coords[axis] + step, 4)
+
+            def pack_ghosts(n, carry, axis=axis, step=step, side=side):
                 far, c = lax.div(n, GCAP), lax.rem(n, GCAP)
-                peer = near * NZ + far if axis == 0 else far * NZ + near
-                packed[axis, step, n] = prolong[numbers[peer, c], axis * half : (axis + 1) * half, :]
+                peer = side * NZ + far if axis == 0 else far * NZ + side
+                packed[axis, step, n] = prolong[wanted[c, 0, peer], axis * half : (axis + 1) * half, :]
                 return carry
 
             lax.fori_loop(0, 4 * GCAP, pack_ghosts, 0)
@@ -197,8 +211,8 @@
                 gsend1.at[axis, behind - 1], grecv1.at[axis, behind - 1], line_peer(axis, behind),
             ).wait_recv()
         at = held.at[axis, behind - 1] if behind else packed.at[axis, 0]
-        near = lax.rem(coords[axis] + 4 - behind, 4)
-        px, pz = (near, z) if axis == 0 else (x, near)
+        side = lax.rem(coords[axis] + 4 - behind, 4)
+        px, pz = (side, z) if axis == 0 else (x, side)
         for s in (1, 2, 3):
             far = lax.rem(coords[1 - axis] + s, 4)
             go(remote(
@@ -215,9 +229,9 @@
         for axis in (0, 1):
             for behind in (0, 1, 2, 3):
                 for s in (1, 2, 3):
-                    near = lax.rem(coords[axis] + 4 - behind, 4)
+                    side = lax.rem(coords[axis] + 4 - behind, 4)
                     far = lax.rem(coords[1 - axis] + 4 - s, 4)
-                    at = ghost_rows(axis, near, far) if axis == 0 else ghost_rows(axis, far, near)
+                    at = ghost_rows(axis, side, far) if axis == 0 else ghost_rows(axis, far, side)
                     remote(
                         at, at, gsend2.at[axis, behind, s - 1], grecv2.at[axis, behind, s - 1], line_peer(1 - axis, s)
                     ).wait_recv()
@@ -233,7 +247,7 @@
             block_copy(c, i, slot).wait()
             applied = []
             for k in range(k0, k1):
-                right = prolong[i] if k == 0 else ghosts[numbers[16 + i, k - 1]]
+                right = prolong[i] if k == 0 else ghosts[near[k - 1, i]]
                 applied.append(
                     jnp.dot(arrived[slot, k - k0], right, preferred_element_type=jnp.float32).astype(jnp.bfloat16)
                 )
@@ -259,14 +273,14 @@
         for step in (2, 1, 3, 0):
             for axis in (0, 1):
                 b = 2 * c + axis
-                near = lax.rem(coords[axis] + step, 4)
-
-                def pack(n, carry, axis=axis, step=step, near=near, b=b):
-                    value = partial[slots[axis, near * LINE + n], 0:span, cuts[axis][0] : cuts[axis][1], :]
+                side = lax.rem(coords[axis] + step, 4)
+
+                def pack(n, carry, axis=axis, step=step, side=side, b=b):
+                    value = partial[slots[axis, side * LINE + n], 0:span, cuts[axis][0] : cuts[axis][1], :]
                     if step:
                         out[b][step - 1, n] = value
                     else:
-                        pool[b][near * LINE + n] = value
+                        pool[b][side * LINE + n] = value
                     return carry
 
                 lax.fori_loop(0, LINE, pack, 0)
@@ -388,20 +402,44 @@
             add_up(0)
         elif c == 2:
             relay(0)
+    own_loads = pad0.at[pl.ds(rows, rows)]
     halo = [
-        remote(loads, low, hsend.at[0], hrecv.at[0], up),
-        remote(loads, high, hsend.at[1], hrecv.at[1], down),
+        remote(own_loads, pad0.at[pl.ds(0, rows)], hsend.at[0], hrecv.at[0], up),
+        remote(own_loads, pad0.at[pl.ds(2 * rows, rows)], hsend.at[1], hrecv.at[1], down),
     ]
     for copy in halo:
         copy.start()
-    for c in range(1, len(CHUNKS)):
+    first_col = (gx * count + gy - 1) * rows
+
+    def padded_row(r, k):
+        return jnp.clip(cols[r, k] - first_col, 0, 3 * rows - 1)
+
+    def multiply_loads(c):
+        k0, k1 = CHUNKS[c]
+
+        def one_row(r, carry):
+            total = product[r]
+            for k in range(k0, k1):
+                total += jnp.dot(coarse[r, k], pad0[padded_row(r, k)], preferred_element_type=jnp.float32)
+            product[r] = total
+            return carry
+
+        lax.fori_loop(0, rows, one_row, 0)
+
+    last = len(CHUNKS) - 1
+    for c in range(1, last + 1):
         add_up(c)
         if c > 1:
             relay(c - 1)
             finish(c - 2)
-    relay(len(CHUNKS) - 1)
-    finish(len(CHUNKS) - 2)
-    finish(len(CHUNKS) - 1)
+    for copy in halo:
+        copy.wait()
+    for c in range(last - 1):
+        multiply_loads(c)
+    relay(last)
+    finish(last - 1)
+    multiply_loads(last - 1)
+    finish(last)
 
     def row_peak(r, top):
         return jnp.maximum(top, jnp.sum(rowsum[r], axis=1, keepdims=True))
@@ -409,20 +447,40 @@
     top = lax.fori_loop(0, rows, row_peak, jnp.zeros((width, 1), jnp.float32))
     peak[0] = jnp.broadcast_to(jnp.max(top, axis=0, keepdims=True), peak.shape[1:])
 
-    base = 0
-    for stage, peers in enumerate((lines[:3], lines[3:], across)):
-        copies = []
-        for n, peer in enumerate(peers):
-            copy = remote(peak.at[stage], peaks.at[base + n], psend.at[base + n], precv.at[base + n], peer)
+    def ask(stage, base, peers):
+        copies = [
+            remote(peak.at[stage], peaks.at[base + n], psend.at[base + n], precv.at[base + n], peer)
+            for n, peer in enumerate(peers)
+        ]
+        for copy in copies:
             copy.start()
-            copies.append(copy)
+        return copies
+
+    def settle_peak(stage, base, copies):
         for copy in copies:
             copy.wait()
         top = peak[stage]
-        for n in range(len(peers)):
+        for n in range(len(copies)):
             top = jnp.maximum(top, peaks[base + n])
         peak[stage + 1] = top
-        base += len(peers)
+
+    asked = ask(0, 0, lines[3:])
+    multiply_loads(last)
+
+    def narrow(r, carry):
+        product_out[r] = product[r].astype(jnp.bfloat16)
+        return carry
+
+    lax.fori_loop(0, rows, narrow, 0)
+    halo = [
+        remote(product_out, product_in.at[0], hsend.at[2], hrecv.at[2], up),
+        remote(product_out, product_in.at[1], hsend.at[3], hrecv.at[3], down),
+    ]
+    for copy in halo:
+        copy.start()
+    settle_peak(0, 0, asked)
+    settle_peak(1, 3, ask(1, 3, lines[:3]))
+    settle_peak(2, 6, ask(2, 6, across))
 
     largest = peak[3, 0:1, 0:1]
     lower_end = largest / 30.0
@@ -430,60 +488,49 @@
     half_width = (largest - lower_end) / 2.0
     sigma = centre / half_width
     weight = 1.0 / sigma
-
-    def begin(r, carry):
-        value = loads[r].astype(jnp.float32) / centre
+    following = 1.0 / (2.0 * sigma - weight)
+    keep = following * weight
+    gain = 2.0 * following / half_width
+
+    def first_sweep(scaled, scaled_product):
+        right = scaled.astype(jnp.float32) * (1.0 / SCALE)
+        start = right / centre
+        residual = right - (scaled_product.astype(jnp.float32) / centre) * (1.0 / SCALE)
+        update = keep * start + gain * residual
+        return start + update, update
+
+    def own_row(r, carry):
+        value, update = first_sweep(pad0[rows + r], product[r])
         state[r] = value
-        change[r] = value
-        pad0[rows + r] = value.astype(jnp.bfloat16)
+        change[r] = update
+        pad1[rows + r] = value.astype(jnp.bfloat16)
         return carry
 
-    lax.fori_loop(0, rows, begin, 0)
-    for copy in halo:
+    lax.fori_loop(0, rows, own_row, 0)
+    for n, copy in enumerate(halo):
         copy.wait()
 
-    def sides(r, carry):
-        pad0[r] = (low[r].astype(jnp.float32) / centre).astype(jnp.bfloat16)
-        pad0[2 * rows + r] = (high[r].astype(jnp.float32) / centre).astype(jnp.bfloat16)
+        def side_row(r, carry, n=n):
+            value, _ = first_sweep(pad0[2 * n * rows + r], product_in[n, r])
+            pad1[2 * n * rows + r] = value.astype(jnp.bfloat16)
+            return carry
+
+        lax.fori_loop(0, rows, side_row, 0)
+
+    weight = following
+    following = 1.0 / (2.0 * sigma - weight)
+    keep_2 = following * weight
+    gain_2 = 2.0 * following / half_width
+
+    def last_row(r, carry):
+        total = jnp.zeros(state.shape[1:], jnp.float32)
+        for k in range(coarse.shape[1]):
+            total += jnp.dot(coarse[r, k], pad1[padded_row(r, k)], preferred_element_type=jnp.float32)
+        residual = loads[r].astype(jnp.float32) - total
+        smoothed[r] = (state[r] + keep_2 * change[r] + gain_2 * residual).astype(jnp.bfloat16)
         return carry
 
-    lax.fori_loop(0, rows, sides, 0)
-
-    for sweep in range(SWEEPS):
-        pad = (pad0, pad1)[sweep]
-        following = 1.0 / (2.0 * sigma - weight)
-        keep = following * weight
-        gain = 2.0 * following / half_width
-
-        def row(r, carry, pad=pad, keep=keep, gain=gain, sweep=sweep):
-            product = jnp.zeros(state.shape[1:], jnp.float32)
-            for k in range(coarse.shape[1]):
-                product += jnp.dot(
-                    coarse[r, k], pad[numbers[40 + r, k]], preferred_element_type=jnp.float32
-                )
-            residual = loads[r].astype(jnp.float32) - product
-            update = keep * change[r] + gain * residual
-            value = state[r] + update
-            if sweep + 1 < SWEEPS:
-                change[r] = update
-                state[r] = value
-                pad1[rows + r] = value.astype(jnp.bfloat16)
-            else:
-                smoothed[r] = value.astype(jnp.bfloat16)
-            return carry
-
-        lax.fori_loop(0, rows, row, 0)
-        weight = following
-        if sweep + 1 < SWEEPS:
-            own = pad1.at[pl.ds(rows, rows)]
-            copies = [
-                remote(own, pad1.at[pl.ds(0, rows)], hsend.at[2], hrecv.at[2], up),
-                remote(own, pad1.at[pl.ds(2 * rows, rows)], hsend.at[3], hrecv.at[3], down),
-            ]
-            for copy in copies:
-                copy.start()
-            for copy in copies:
-                copy.wait()
+    lax.fori_loop(0, rows, last_row, 0)
     for copy in sent:
         copy.wait_send()
 
@@ -493,28 +540,8 @@
     width = prolong.shape[2]
     rows, _, columns = loads.shape
     count = NX * NZ
-    me = lax.axis_index("gy")
-    device = lax.axis_index("gx") * count + me
-    near_cols = coarse_cols - (device - 1) * rows
-    lane = jnp.arange(128, dtype=jnp.int32)
-    fourfold = jnp.pad(jnp.concatenate([fine_agg] * 4), (0, 128 - 4 * fine_rows))
-    labels = [
-        jnp.where((lane >= at * fine_rows) & (lane < (at + 1) * fine_rows), fourfold, 0)[None]
-        for at in (me // NZ, me % NZ)
-    ]
-
-    def wide(values):
-        return jnp.pad(values, ((0, 0), (0, 128 - values.shape[1])))
-
-    ints = jnp.concatenate(
-        [
-            jnp.broadcast_to(balance[0, 0][:, None], (count, 128)),
-            *labels,
-            jnp.zeros((6, 128), jnp.int32),
-            wide(ghost_send[0, 0]),
-            wide(neighbour),
-            wide(near_cols),
-        ]
+    numbers = (
+        neighbour.T, ghost_send.transpose(0, 3, 1, 2)[0], fine_agg[None], balance[0, 0][None], coarse_cols
     )
     bf16, f32 = jnp.bfloat16, jnp.float32
     n_b = 2 * len(CHUNKS)
@@ -525,18 +552,21 @@
     bufs += [VMEM((4, rows, *n), bf16) for n in shapes]
     bufs += [VMEM((2, rows // 2, *n), bf16) for n in shapes]
     bufs += [VMEM((2, rows, *n), bf16) for n in shapes]
-    vmem = pl.BlockSpec(memory_space=VMEM)
+    vmem, anywhere = pl.BlockSpec(memory_space=VMEM), pl.BlockSpec(memory_space=pl.ANY)
     return pl.pallas_call(
         functools.partial(kernel, n_gx),
         out_shape=(
             jax.ShapeDtypeStruct((rows, pieces, width, width), bf16),
             jax.ShapeDtypeStruct((rows, width, columns), bf16),
         ),
-        in_specs=[pl.BlockSpec(memory_space=pl.ANY), vmem, vmem, vmem],
+        in_specs=[anywhere, vmem, anywhere, anywhere, vmem, vmem, anywhere, vmem],
         out_specs=(vmem, vmem),
         scratch_shapes=[
-            SMEM((ints.shape[0] - TABLE, 128), jnp.int32),
-            VMEM((NX, NZ, TABLE, 128), jnp.int32),
+            SMEM((pieces - 1, fine_rows), jnp.int32),
+            SMEM((GCAP, 1, count), jnp.int32),
+            SMEM((rows, pieces), jnp.int32),
+            VMEM((8, 128), jnp.int32),
+            VMEM((NX, NZ, 8, 128), jnp.int32),
             VMEM((8, 128), jnp.int32),
             SMEM((8, 128), jnp.int32),
             VMEM((2, 4, 4 * GCAP, order // 2, width), bf16),
@@ -544,16 +574,17 @@
             VMEM((fine_rows + count * GCAP, order, width), bf16),
             VMEM((AHEAD, SPAN, order, order), bf16),
             VMEM((fine_rows, SPAN, width, width), bf16),
-            VMEM((rows, width, columns), bf16),
-            VMEM((rows, width, columns), bf16),
             VMEM((3 * rows, width, columns), bf16),
             VMEM((3 * rows, width, columns), bf16),
+            VMEM((rows, width, columns), f32),
+            VMEM((rows, width, columns), bf16),
+            VMEM((2, rows, width, columns), bf16),
             VMEM((rows, width, columns), f32),
             VMEM((rows, width, columns), f32),
             VMEM((rows, width, width), f32),
             VMEM((4, 8, 128), f32),
             VMEM((peers, 8, 128), f32),
-            DMA((4,)), DMA((AHEAD,)),
+            DMA((8,)), DMA((AHEAD,)),
             DMA((3,)), DMA((3,)), DMA((4, 3)), DMA((4, 3)),
             DMA((2, 3)), DMA((2, 3)), DMA((2, 4, 3)), DMA((2, 4, 3)), DMA((2, 4)),
             DMA((n_b, 3)), DMA((n_b, 3)),
@@ -569,7 +600,7 @@
             bytes_accessed=2 * fine_rows * pieces * order * order,
             transcendentals=0,
         ),
-    )(a_blocks, prolong, ints, loads)
+    )(a_blocks, prolong, *numbers, loads)
 
 
 def solution(mesh):

time: 202 us -> 185 us (0.916)
  Pallas kernels: 191 us -> 180 us
  local copies, waits for them, and re-layouts: 9.06 us -> 3.8 us
    pallas_call x1, Pallas kernels: 191 us -> 180 us  [per_device(): pl.pallas_call(functools.partial(kernel, n_gx), out_shape=(jax.ShapeDtype...]
    concatenate x1 -> x0, local copies, waits for them, and re-layouts: 3 us -> none  [per_device(): jnp.concatenate([jnp.broadcast_to(balance[0, 0][:, None], (count, 128)),...]
    unnamed x5 -> x4, local copies, waits for them, and re-layouts: 4.56 us -> 3.8 us
where the time goes in v3:
time: 185 us
  Pallas kernels  180 us (97%)
  local copies, waits for them, and re-layouts  3.8 us (2%)
    pallas_call x1, Pallas kernels, per_device(): pl.pallas_call(functools.partial(kernel, n_gx), out_shape=(jax.ShapeDtype...  180 us
    unnamed x4, local copies, waits for them, and re-layouts  3.8 us

profile of v3, /device:TPU:1, one launch (start us, length us, event | category | flops | bytes accessed | tf_op | source)
XLA Modules:
  0.0 184.9 jit_solution(1059394368682571662)
XLA Ops:
  0.6 180.5 %shard_map.95 = (bf16[8,7,128,128]{3,2,1,0:T(8,128)(2,1)}, bf16[8,128,256]{2,1,0:T(8,128)(2,1)}) custom-call(bf16[24,7,256,256]{3,2,1,0:T(8,128)(2,1)} %blocks.1, bf16[24,256,128]{2,1,0:T(8,128)(2,1)} %prolong.1, s32[6,24]{1,0:T(8,128)} %bitcast.6, s32[3,1,16]{2,1,0:T(1,128)} %bitcast.7, s32[1,24]{1,0:T(1,128)} %bitcast.8, s32[1,16]{1,0:T(1,128)} %bitcast.9, ...), custom_call_target="tpu_custom_call" | custom-call | flops 4227858432 | bytes 22020096 | tf_op jit(solution)/shard_map/pallas_call | solution.py:556
  181.1 0.0 copy-start
  181.1 3.0 %copy.12 = bf16[8,7,128,128]{3,2,1,0:T(8,128)(2,1)} copy(bf16[8,7,128,128]{3,2,1,0:T(8,128)(2,1)} %get-tuple-element.4) | data formatting | bytes 3670016
  184.1 0.0 copy-done
  184.1 0.8 copy.13
Async XLA Ops:
  181.1 3.0 %copy-start = (bf16[8,128,256]{2,1,0:T(8,128)(2,1)S(1)}, bf16[8,128,256]{2,1,0:T(8,128)(2,1)}, u32[]{:S(2)}) copy-start(bf16[8,128,256]{2,1,0:T(8,128)(2,1)} %get-tuple-element.5) | copy-start | bytes 1572868

commit v4 on v3

--- a/solution.py
+++ b/solution.py
@@ -14,6 +14,7 @@
 LINE = 12
 CHUNKS = ((0, 1), (1, 2), (2, 4), (4, 6), (6, 7))
 SPAN = max(k1 - k0 for k0, k1 in CHUNKS)
+ROWS = 4
 AHEAD = 8
 SCALE = 1.0 / 256.0
 VMEM = pltpu.VMEM
@@ -51,6 +52,15 @@
     return ((0, cut), (cut, width))
 
 
+def steps(count, unroll, body):
+    def several(n, carry):
+        for m in range(unroll):
+            body(n * unroll + m)
+        return carry
+
+    lax.fori_loop(0, count // unroll, several, 0)
+
+
 def index_tables(tables, coarse_rows, coords):
     shape = (128, 128)
     lane, sub = (lax.broadcasted_iota(jnp.int32, shape, d) for d in (1, 0))
@@ -66,6 +76,10 @@
         picked = mask.astype(jnp.int32) if values is None else jnp.where(mask, values, 0)
         return jnp.sum(picked, axis=0, keepdims=True)
 
+    given = jnp.concatenate(
+        [tables[owner // NZ, owner % NZ, 1:2, :] for owner in range(NX * NZ)] + [jnp.zeros((112, 128), jnp.int32)]
+    )
+    given = jnp.transpose(given)[0:16]
     lane_row = lane[0:1]
     source, source_down = quarter(lane), quarter(sub)
     source_row = source[0:1]
@@ -78,8 +92,7 @@
         found = jnp.zeros((16, 128), jnp.int32)
         for owner in range(NX * NZ):
             slot_of = owner * 16 + lax.broadcasted_iota(jnp.int32, (16, 128), 0)
-            given = down(tables[owner // NZ, owner % NZ, 1:2, :])[0:16]
-            found += jnp.where(slot_of == label, given, 0)
+            found += jnp.where(slot_of == label, given[:, owner : owner + 1], 0)
         target = jnp.sum(found, axis=0, keepdims=True)
         device = lax.shift_right_logical(target, bits)
         row = target & (coarse_rows - 1)
@@ -173,13 +186,12 @@
         for axis in (0, 1):
             side = lax.rem(coords[axis] + step, 4)
 
-            def pack_ghosts(n, carry, axis=axis, step=step, side=side):
+            def pack_ghosts(n, axis=axis, step=step, side=side):
                 far, c = lax.div(n, GCAP), lax.rem(n, GCAP)
                 peer = side * NZ + far if axis == 0 else far * NZ + side
                 packed[axis, step, n] = prolong[wanted[c, 0, peer], axis * half : (axis + 1) * half, :]
-                return carry
-
-            lax.fori_loop(0, 4 * GCAP, pack_ghosts, 0)
+
+            steps(4 * GCAP, 6, pack_ghosts)
             if step:
                 go(remote(
                     packed.at[axis, step], held.at[axis, step - 1],
@@ -242,9 +254,8 @@
     def multiply(c):
         k0, k1 = CHUNKS[c]
 
-        def one_row(i, carry):
+        def one_row(i):
             slot = lax.rem(i, AHEAD)
-            block_copy(c, i, slot).wait()
             applied = []
             for k in range(k0, k1):
                 right = prolong[i] if k == 0 else ghosts[near[k - 1, i]]
@@ -258,13 +269,21 @@
             for k in range(k1 - k0):
                 partial[i, k] = value[:, k * width : (k + 1) * width]
 
-            @pl.when(i + AHEAD < fine_rows)
+        def some_rows(n, carry):
+            first = n * ROWS
+            for m in range(ROWS):
+                block_copy(c, first + m, lax.rem(first + m, AHEAD)).wait()
+            for m in range(ROWS):
+                one_row(first + m)
+
+            @pl.when(first + AHEAD < fine_rows)
             def _():
-                block_copy(c, i + AHEAD, slot).start()
+                for m in range(ROWS):
+                    block_copy(c, first + AHEAD + m, lax.rem(first + m, AHEAD)).start()
 
             return carry
 
-        lax.fori_loop(0, fine_rows, one_row, 0)
+        lax.fori_loop(0, fine_rows // ROWS, some_rows, 0)
         if c + 1 < len(CHUNKS):
             fetch(c + 1)
 
@@ -275,15 +294,14 @@
                 b = 2 * c + axis
                 side = lax.rem(coords[axis] + step, 4)
 
-                def pack(n, carry, axis=axis, step=step, side=side, b=b):
+                def pack(n, axis=axis, step=step, side=side, b=b):
                     value = partial[slots[axis, side * LINE + n], 0:span, cuts[axis][0] : cuts[axis][1], :]
                     if step:
                         out[b][step - 1, n] = value
                     else:
                         pool[b][side * LINE + n] = value
-                    return carry
-
-                lax.fori_loop(0, LINE, pack, 0)
+
+                steps(LINE, 6, pack)
                 if step:
                     go(remote(
                         out[b].at[step - 1], pool[b].at[pl.ds(coords[axis] * LINE, LINE)],
@@ -305,7 +323,7 @@
             for step in (2, 1, 3, 0):
                 far = lax.rem(coords[1 - axis] + step, 4)
 
-                def merge(r, carry, axis=axis, b=b, step=step, far=far):
+                def merge(r, axis=axis, b=b, step=step, far=far):
                     at = (far * rows + r) * 3
                     terms = [slots[2 + axis, at + n] for n in range(3)]
                     for k in range(span):
@@ -313,9 +331,8 @@
                         total += pool[b][terms[1], k].astype(jnp.float32)
                         total += pool[b][terms[2], k].astype(jnp.float32)
                         sums[b][step, r, k] = total.astype(jnp.bfloat16)
-                    return carry
-
-                lax.fori_loop(0, rows, merge, 0)
+
+                steps(rows, 4, merge)
                 if step == 2:
                     for n, s in enumerate((1, 3)):
                         go(remote(
@@ -340,14 +357,13 @@
                     send2.at[b, n], recv2.at[b, n], line_peer(1 - axis, step),
                 ).wait_recv()
 
-                def take(r, carry, b=b, n=n, step=step):
+                def take(r, b=b, n=n, step=step):
                     for k in range(span):
                         total = sums[b][step, n * hrows + r, k].astype(jnp.float32)
                         total += passing[b][n, r, k].astype(jnp.float32)
                         sums[b][step, n * hrows + r, k] = total.astype(jnp.bfloat16)
-                    return carry
-
-                lax.fori_loop(0, hrows, take, 0)
+
+                steps(hrows, 4, take)
                 part = pl.ds(n * hrows, hrows)
                 go(remote(
                     sums[b].at[step, part], back[b].at[n, part],
@@ -367,7 +383,7 @@
                         send.at[b, n], recv.at[b, n], line_peer(1 - axis, step),
                     ).wait_recv()
 
-            def settle(r, carry, b=b, lo=lo, hi=hi):
+            def settle(r, b=b, lo=lo, hi=hi):
                 size = jnp.zeros((hi - lo, width), jnp.float32)
                 for k in range(k1 - k0):
                     total = sums[b][0, r, k].astype(jnp.float32)
@@ -377,16 +393,15 @@
                     coarse[r, k0 + k, lo:hi, :] = rounded
                     size += jnp.abs(rounded.astype(jnp.float32))
                 rowsum[r, lo:hi, :] = size if c == 0 else rowsum[r, lo:hi, :] + size
-                return carry
-
-            lax.fori_loop(0, rows, settle, 0)
-
+
+            steps(rows, 2, settle)
+
+    forward_ghosts(0, 0)
+    forward_ghosts(0, 1)
     multiply(0)
     for copy in table_in:
         copy.wait_recv()
     slots_v[...] = index_tables(tables, rows, coords)
-    forward_ghosts(0, 0)
-    forward_ghosts(0, 1)
     slot_copy = pltpu.make_async_copy(slots_v, slots, near_sem.at[3])
     slot_copy.start()
     slot_copy.wait()
@@ -417,14 +432,13 @@
     def multiply_loads(c):
         k0, k1 = CHUNKS[c]
 
-        def one_row(r, carry):
+        def one_row(r):
             total = product[r]
             for k in range(k0, k1):
                 total += jnp.dot(coarse[r, k], pad0[padded_row(r, k)], preferred_element_type=jnp.float32)
             product[r] = total
-            return carry
-
-        lax.fori_loop(0, rows, one_row, 0)
+
+        steps(rows, 4, one_row)
 
     last = len(CHUNKS) - 1
     for c in range(1, last + 1):
@@ -522,15 +536,14 @@
     keep_2 = following * weight
     gain_2 = 2.0 * following / half_width
 
-    def last_row(r, carry):
+    def last_row(r):
         total = jnp.zeros(state.shape[1:], jnp.float32)
         for k in range(coarse.shape[1]):
             total += jnp.dot(coarse[r, k], pad1[padded_row(r, k)], preferred_element_type=jnp.float32)
         residual = loads[r].astype(jnp.float32) - total
         smoothed[r] = (state[r] + keep_2 * change[r] + gain_2 * residual).astype(jnp.bfloat16)
-        return carry
-
-    lax.fori_loop(0, rows, last_row, 0)
+
+    steps(rows, 2, last_row)
     for copy in sent:
         copy.wait_send()
 

time: 185 us -> 176 us (0.951)
  Pallas kernels: 180 us -> 171 us
    pallas_call x1, Pallas kernels: 180 us -> 171 us  [per_device(): pl.pallas_call(functools.partial(kernel, n_gx), out_shape=(jax.ShapeDtype...]
where the time goes in v4:
time: 176 us
  Pallas kernels  171 us (97%)
  local copies, waits for them, and re-layouts  3.8 us (2%)
    pallas_call x1, Pallas kernels, per_device(): pl.pallas_call(functools.partial(kernel, n_gx), out_shape=(jax.ShapeDtype...  171 us
    unnamed x4, local copies, waits for them, and re-layouts  3.8 us

profile of v4, /device:TPU:1, one launch (start us, length us, event | category | flops | bytes accessed | tf_op | source)
XLA Modules:
  0.0 175.9 jit_solution(2314882816806646100)
XLA Ops:
  0.6 171.4 %shard_map.95 = (bf16[8,7,128,128]{3,2,1,0:T(8,128)(2,1)}, bf16[8,128,256]{2,1,0:T(8,128)(2,1)}) custom-call(bf16[24,7,256,256]{3,2,1,0:T(8,128)(2,1)} %blocks.1, bf16[24,256,128]{2,1,0:T(8,128)(2,1)} %prolong.1, s32[6,24]{1,0:T(8,128)} %bitcast.6, s32[3,1,16]{2,1,0:T(1,128)} %bitcast.7, s32[1,24]{1,0:T(1,128)} %bitcast.8, s32[1,16]{1,0:T(1,128)} %bitcast.9, ...), custom_call_target="tpu_custom_call" | custom-call | flops 4227858432 | bytes 22020096 | tf_op jit(solution)/shard_map/pallas_call | solution.py:569
  172.1 0.0 copy-start
  172.1 3.0 %copy.12 = bf16[8,7,128,128]{3,2,1,0:T(8,128)(2,1)} copy(bf16[8,7,128,128]{3,2,1,0:T(8,128)(2,1)} %get-tuple-element.4) | data formatting | bytes 3670016
  175.1 0.0 copy-done
  175.1 0.8 copy.13
Async XLA Ops:
  172.1 3.0 %copy-start = (bf16[8,128,256]{2,1,0:T(8,128)(2,1)S(1)}, bf16[8,128,256]{2,1,0:T(8,128)(2,1)}, u32[]{:S(2)}) copy-start(bf16[8,128,256]{2,1,0:T(8,128)(2,1)} %get-tuple-element.5) | copy-start | bytes 1572868

commit v5 on v4

--- a/solution.py
+++ b/solution.py
@@ -38,7 +38,10 @@
     barrier = pltpu.get_barrier_semaphore()
     for peer in peers:
         pl.semaphore_signal(barrier, 1, device_id=peer, device_id_type=MESH)
-    pl.semaphore_wait(barrier, len(peers))
+
+
+def meet(peers):
+    pl.semaphore_wait(pltpu.get_barrier_semaphore(), len(peers))
 
 
 def remote(src, dst, send, recv, peer):
@@ -151,6 +154,7 @@
         for n in range(AHEAD):
             block_copy(c, n, n).start()
 
+    greet(lines + [up, down] + across)
     own_numbers = [
         pltpu.make_async_copy(source, held_in, near_sem.at[4 + n])
         for n, (source, held_in) in enumerate(((sends, wanted), (neighbours, near), (columns, cols)))
@@ -165,38 +169,33 @@
     own_table = pltpu.make_async_copy(table, tables.at[x, z], near_sem.at[2])
     own_table.start()
     fetch(0)
-
-    def scale_row(r, carry):
-        pad0[rows + r] = (loads[r].astype(jnp.float32) * SCALE).astype(jnp.bfloat16)
-        product[r] = jnp.zeros(product.shape[1:], jnp.float32)
-        return carry
-
-    lax.fori_loop(0, rows, scale_row, 0)
-    greet(lines + [up, down] + across)
+    for copy in own_numbers:
+        copy.wait()
+
+    for step in (2, 1, 3, 0):
+        for axis in (0, 1):
+            side = lax.rem(coords[axis] + step, 4)
+
+            def pack_ghosts(n, axis=axis, step=step, side=side):
+                far, c = lax.div(n, GCAP), lax.rem(n, GCAP)
+                peer = side * NZ + far if axis == 0 else far * NZ + side
+                packed[axis, step, n] = prolong[wanted[c, 0, peer], axis * half : (axis + 1) * half, :]
+
+            steps(4 * GCAP, 6, pack_ghosts)
+
+    meet(lines + [up, down] + across)
 
     first_tables = [
         remote(table, tables.at[x, z], tsend1.at[s - 1], trecv1.at[s - 1], line_peer(0, s)) for s in (1, 2, 3)
     ]
     for copy in first_tables:
         go(copy)
-    for copy in own_numbers:
-        copy.wait()
-
-    for step in (2, 1, 3, 0):
+    for step in (2, 1, 3):
         for axis in (0, 1):
-            side = lax.rem(coords[axis] + step, 4)
-
-            def pack_ghosts(n, axis=axis, step=step, side=side):
-                far, c = lax.div(n, GCAP), lax.rem(n, GCAP)
-                peer = side * NZ + far if axis == 0 else far * NZ + side
-                packed[axis, step, n] = prolong[wanted[c, 0, peer], axis * half : (axis + 1) * half, :]
-
-            steps(4 * GCAP, 6, pack_ghosts)
-            if step:
-                go(remote(
-                    packed.at[axis, step], held.at[axis, step - 1],
-                    gsend1.at[axis, step - 1], grecv1.at[axis, step - 1], line_peer(axis, step),
-                ))
+            go(remote(
+                packed.at[axis, step], held.at[axis, step - 1],
+                gsend1.at[axis, step - 1], grecv1.at[axis, step - 1], line_peer(axis, step),
+            ))
 
     own_table.wait()
     table_in = []
@@ -398,16 +397,22 @@
 
     forward_ghosts(0, 0)
     forward_ghosts(0, 1)
+    def scale_row(r, carry):
+        pad0[rows + r] = (loads[r].astype(jnp.float32) * SCALE).astype(jnp.bfloat16)
+        product[r] = jnp.zeros(product.shape[1:], jnp.float32)
+        return carry
+
+    lax.fori_loop(0, rows, scale_row, 0)
     multiply(0)
+    for behind in (1, 3, 2):
+        for axis in (0, 1):
+            forward_ghosts(behind, axis)
     for copy in table_in:
         copy.wait_recv()
     slots_v[...] = index_tables(tables, rows, coords)
     slot_copy = pltpu.make_async_copy(slots_v, slots, near_sem.at[3])
     slot_copy.start()
     slot_copy.wait()
-    for behind in (1, 3, 2):
-        for axis in (0, 1):
-            forward_ghosts(behind, axis)
     scatter(0)
     wait_ghosts()
     for c in range(1, len(CHUNKS)):

time: 176 us -> 175 us (level)
    pallas_call x1, Pallas kernels: 171 us -> 170 us  [per_device(): pl.pallas_call(functools.partial(kernel, n_gx), out_shape=(jax.ShapeDtype...]
where the time goes in v5:
time: 175 us; the launch traced here: 174 us
  Pallas kernels  170 us (97%)
  local copies, waits for them, and re-layouts  3.8 us (2%)
    pallas_call x1, Pallas kernels, per_device(): pl.pallas_call(functools.partial(kernel, n_gx), out_shape=(jax.ShapeDtype...  170 us
    unnamed x4, local copies, waits for them, and re-layouts  3.8 us

profile of v5, /device:TPU:1, one launch (start us, length us, event | category | flops | bytes accessed | tf_op | source)
XLA Modules:
  0.0 174.0 jit_solution(5173955995953269856)
XLA Ops:
  0.6 169.5 %shard_map.95 = (bf16[8,7,128,128]{3,2,1,0:T(8,128)(2,1)}, bf16[8,128,256]{2,1,0:T(8,128)(2,1)}) custom-call(bf16[24,7,256,256]{3,2,1,0:T(8,128)(2,1)} %blocks.1, bf16[24,256,128]{2,1,0:T(8,128)(2,1)} %prolong.1, s32[6,24]{1,0:T(8,128)} %bitcast.6, s32[3,1,16]{2,1,0:T(1,128)} %bitcast.7, s32[1,24]{1,0:T(1,128)} %bitcast.8, s32[1,16]{1,0:T(1,128)} %bitcast.9, ...), custom_call_target="tpu_custom_call" | custom-call | flops 4227858432 | bytes 22020096 | tf_op jit(solution)/shard_map/pallas_call | solution.py:574
  170.2 0.0 copy-start
  170.2 3.0 %copy.12 = bf16[8,7,128,128]{3,2,1,0:T(8,128)(2,1)} copy(bf16[8,7,128,128]{3,2,1,0:T(8,128)(2,1)} %get-tuple-element.4) | data formatting | bytes 3670016
  173.2 0.0 copy-done
  173.2 0.8 copy.13
Async XLA Ops:
  170.2 3.0 %copy-start = (bf16[8,128,256]{2,1,0:T(8,128)(2,1)S(1)}, bf16[8,128,256]{2,1,0:T(8,128)(2,1)}, u32[]{:S(2)}) copy-start(bf16[8,128,256]{2,1,0:T(8,128)(2,1)} %get-tuple-element.5) | copy-start | bytes 1572868
